TPU v7x, 256 devices: a whole 4x4x8 slice. The times are simulated.
256 devices in a mesh: frames: 64 (over x, z, core), mp: 4 (over y).
Axes of the slice: x: 4, y: 4, z: 8, core: 2. Of those that a mesh axis runs over, the one named last changes fastest.
Arguments:
- frames: bfloat16 [1024, 64, 1152], P('frames'), may hold values from -6 to 6
- keyframes: int32 [256, 16], P('frames'), may hold values from 0 to 1023, as said below
- query_states: bfloat16 [256, 32, 768], P('frames'), may hold values from -6 to 6
- w_query: bfloat16 [768, 768], P(None, 'mp'), may hold values from -1 to 1
- w_key: bfloat16 [1152, 768], P(None, 'mp'), may hold values from -1 to 1
- w_value: bfloat16 [1152, 768], P(None, 'mp'), may hold values from -0.1875 to 0.1875
- w_out: bfloat16 [768, 768], P('mp'), may hold values from -0.21875 to 0.21875
- out_grad: bfloat16 [256, 32, 768], P('frames'), may hold values from -6 to 6
Outputs:
- attended: bfloat16 [256, 32, 768], P('frames', None, 'mp')
- query_grad: bfloat16 [256, 32, 768], P('frames', None, 'mp')
- frame_grad: bfloat16 [1024, 64, 1152], P('frames', None, 'mp')
Inputs may be any that keep to these rules, and one draw needn't show every extreme that they name: `keyframes`: each entry names a frame. The 64 picks of the questions of one index of frames fall on owners (frame // 16) in groups of exactly 2: every owner gets either 0 or 2 of them.
All inputs are finite; a program needn't handle non-finite values.
Results may differ from a plain program's by a relative error of at most 0.04.
The roundings to bfloat16 on the way count: a program that leaves them out, or rounds other values in their place, can miss the bound.
Values may be sent and summed in bfloat16 or wider, within the bound.
No kernel may reach another device: no remote copies, remote signals or barrier semaphores. Data moves between devices by JAX's collectives and lax.ppermute only.
A program may use at most 128 MiB of HBM per device.

v0:
```python
import jax
import jax.numpy as jnp
from jax import lax
from jax.sharding import PartitionSpec as P

HEAD_DIM = 64


def body(frames, keyframes, query_states, w_query, w_key, w_value, w_out, out_grad):
    owners = lax.axis_size("frames")
    fr_count = frames.shape[0]
    tok = frames.shape[1]
    width = frames.shape[2]
    quests = keyframes.shape[0]
    nq = query_states.shape[1]
    head_cols = w_key.shape[1]
    heads_here = head_cols // HEAD_DIM
    scale = HEAD_DIM ** (-0.5)
    picks = keyframes.reshape(-1)
    count = picks.shape[0]
    cap = max(2, count // owners)
    owner = picks // fr_count
    local = picks % fr_count
    position = jnp.arange(count)
    same = owner[:, None] == owner[None, :]
    earlier = position[None, :] < position[:, None]
    rank = jnp.sum(jnp.logical_and(same, earlier), axis=1)
    requests = jnp.zeros((owners, cap), jnp.int32).at[owner, rank].set(local + 1)
    incoming = lax.all_to_all(requests, "frames", split_axis=0, concat_axis=0, tiled=True)
    valid = incoming > 0
    rows_index = jnp.maximum(incoming - 1, 0)
    w_both = jnp.concatenate([w_key, w_value], axis=1)
    part = width // lax.axis_size("mp")
    slab = lax.dynamic_slice_in_dim(frames, lax.axis_index("mp") * part, part, 2)
    outgoing = jnp.where(valid[:, :, None, None], slab[rows_index], jnp.zeros((), jnp.bfloat16))
    returned = lax.all_to_all(outgoing, "frames", split_axis=0, concat_axis=0, tiled=True)
    chosen = returned[owner, rank].reshape(count * tok, part)
    both = jnp.dot(
        lax.all_gather(chosen, "mp", axis=1, tiled=True), w_both, preferred_element_type=jnp.float32
    )
    both = both.astype(jnp.bfloat16).reshape(count, tok, 2 * head_cols)
    keys = both[:, :, :head_cols].reshape(quests, count // quests * tok, heads_here, HEAD_DIM)
    values = both[:, :, head_cols:].reshape(quests, count // quests * tok, heads_here, HEAD_DIM)
    queries = jnp.dot(
        query_states.reshape(quests * nq, -1), w_query, preferred_element_type=jnp.float32
    )
    queries = queries.astype(jnp.bfloat16).reshape(quests, nq, heads_here, HEAD_DIM)
    scores = (
        jnp.einsum("qnhd,qkhd->qhnk", queries, keys, preferred_element_type=jnp.float32) * scale
    )
    probs = jax.nn.softmax(scores, axis=-1)
    weights = probs.astype(jnp.bfloat16)
    mixed = jnp.einsum("qhnk,qkhd->qnhd", weights, values, preferred_element_type=jnp.float32)
    mixed = mixed.astype(jnp.bfloat16).reshape(quests * nq, head_cols)
    out_terms = jnp.dot(mixed, w_out, preferred_element_type=jnp.float32).reshape(quests, nq, -1)
    attended = lax.psum_scatter(
        out_terms.astype(jnp.bfloat16), "mp", scatter_dimension=2, tiled=True
    )
    d_mixed = jnp.einsum(
        "rc,hc->rh", out_grad.reshape(quests * nq, -1), w_out, preferred_element_type=jnp.float32
    )
    d_mixed = d_mixed.astype(jnp.bfloat16).reshape(quests, nq, heads_here, HEAD_DIM)
    d_probs = jnp.einsum("qnhd,qkhd->qhnk", d_mixed, values, preferred_element_type=jnp.float32)
    d_scores = probs * (d_probs - jnp.sum(probs * d_probs, axis=-1, keepdims=True)) * scale
    d_scores = d_scores.astype(jnp.bfloat16)
    d_queries = jnp.einsum("qhnk,qkhd->qnhd", d_scores, keys, preferred_element_type=jnp.float32)
    d_queries = d_queries.astype(jnp.bfloat16).reshape(quests * nq, head_cols)
    query_terms = jnp.einsum("rh,ch->rc", d_queries, w_query, preferred_element_type=jnp.float32)
    query_grad = lax.psum_scatter(
        query_terms.reshape(quests, nq, -1).astype(jnp.bfloat16),
        "mp",
        scatter_dimension=2,
        tiled=True,
    )
    d_keys = jnp.einsum(
        "qhnk,qnhd->qkhd", d_scores, queries, preferred_element_type=jnp.float32
    ).astype(jnp.bfloat16)
    d_values = jnp.einsum(
        "qhnk,qnhd->qkhd", weights, d_mixed, preferred_element_type=jnp.float32
    ).astype(jnp.bfloat16)
    d_both = jnp.concatenate(
        [d_keys.reshape(count, tok, head_cols), d_values.reshape(count, tok, head_cols)], axis=-1
    )
    send_back = (
        jnp.zeros((owners, cap, tok, 2 * head_cols), jnp.bfloat16).at[owner, rank].set(d_both)
    )
    arrived = lax.all_to_all(send_back, "frames", split_axis=0, concat_axis=0, tiled=True)
    target = jnp.where(valid, rows_index, -1).reshape(-1)
    one_hot = (target[None, :] == jnp.arange(fr_count)[:, None]).astype(jnp.bfloat16)
    summed = jnp.dot(
        one_hot,
        arrived.reshape(owners * cap, tok * 2 * head_cols),
        preferred_element_type=jnp.float32,
    )
    summed = summed.astype(jnp.bfloat16).reshape(fr_count * tok, 2 * head_cols)
    grad_terms = jnp.einsum("rh,ch->rc", summed, w_both, preferred_element_type=jnp.float32)
    frame_grad = lax.psum_scatter(
        grad_terms.reshape(fr_count, tok, width).astype(jnp.bfloat16),
        "mp",
        scatter_dimension=2,
        tiled=True,
    )
    return (attended, query_grad, frame_grad)


def solution(mesh):
    placed = (
        P("frames", None, None),
        P("frames", None),
        P("frames", None, None),
        P(None, "mp"),
        P(None, "mp"),
        P(None, "mp"),
        P("mp", None),
        P("frames", None, None),
    )
    return jax.shard_map(
        body,
        mesh=mesh,
        in_specs=placed,
        out_specs=(P("frames", None, "mp"), P("frames", None, "mp"), P("frames", None, "mp")),
        check_vma=False,
    )
```

profile of v0, /device:TPU:1, one launch (start us, length us, event | category | flops | bytes accessed | tf_op | source)
XLA Modules:
  0.0 608.3 jit_solution(11181687715305978329)
XLA Ops:
  7.2 0.9 reshape.234
  8.1 0.8 reshape.233
  8.9 0.2 convert_reduce_fusion
  9.1 3.5 scatter_fusion
  12.6 0.7 copy.108
  13.3 13.0 %all-to-all-start = ((s32[64,1,2]{2,1,0:T(1,128)}), s32[64,1,2]{2,1,0:T(1,128)S(1)}, u32[]{:S(2)}, u32[]{:S(2)}) async-start(s32[64,1,2]{2,1,0:T(1,128)} %copy.108), calls=%async_computation | async-start | bytes 65536 | tf_op jit(solution)/shard_map/all_to_all | solution.py:29
  26.4 0.3 constant_dynamic-slice_fusion
  26.7 8.8 %all-to-all-done = s32[64,1,2]{2,1,0:T(1,128)S(1)} async-done(((s32[64,1,2]{2,1,0:T(1,128)}), s32[64,1,2]{2,1,0:T(1,128)S(1)}, u32[]{:S(2)}, u32[]{:S(2)}) %all-to-all-start) | async-done | bytes 544 | tf_op jit(solution)/shard_map/all_to_all | solution.py:29
  35.8 0.2 select_reduce_fusion
  36.2 4.1 gather_fusion
  40.2 3.4 broadcast_select_fusion
  43.7 146.1 %all_to_all.19 = bf16[64,2,64,288]{3,2,1,0:T(8,128)(2,1)} all-to-all(bf16[64,2,64,288]{3,2,1,0:T(8,128)(2,1)S(1)} %broadcast_select_fusion), channel_id=1, replica_groups=mesh['frames'=64,'mp'=4] {'frames'}, dimensions={0} | all-to-all | bytes 9437184 | tf_op jit(solution)/shard_map/all_to_all | solution.py:36
  189.7 5.5 gather_fusion.1
  195.2 4.5 copy.111
  199.8 0.9 copy-done.4
  200.8 0.2 convolution_convert_fusion.8
  201.3 0.2 convolution_convert_fusion.9
  201.9 0.2 copy.112
  202.2 0.2 copy.113
  202.4 88.7 %all-gather.2.cloned.1.call-done = bf16[4096,1152]{0,1:T(8,128)(2,1)} async-done(((bf16[4096,288]{0,1:T(8,128)(2,1)}), bf16[4096,1152]{0,1:T(8,128)(2,1)}) %all-gather.2.cloned.1.call-update) | async-done | bytes 9437200 | tf_op jit(solution)/shard_map/all_gather | solution.py:39
  291.1 8.2 %convolution_convert_fusion.1 = bf16[4096,384]{1,0:T(8,128)(2,1)S(1)} fusion(bf16[4096,1152]{0,1:T(8,128)(2,1)} %all-gather.2.cloned.1.call-done, bf16[1152,192]{1,0:T(8,128)(2,1)S(1)} %copy.113, bf16[1152,192]{1,0:T(8,128)(2,1)S(1)} %copy.112), kind=kOutput, calls=%fused_computation.9 | convolution fusion | flops 3627220992 | bytes 13467648 | tf_op jit(solution)/shard_map/dot_general | solution.py:38
  299.4 2.6 fusion.41
  302.0 8.5 %reshape.289 = bf16[4,1024,3,64]{3,2,1,0:T(4,128)(2,1)} reshape(bf16[64,64,192]{2,1,0:T(8,128)(2,1)} %get-tuple-element.7) | data formatting | bytes 3145728 | tf_op jit(solution)/shard_map/reshape | solution.py:42
  310.4 6.7 %copy.118 = bf16[4,1024,3,64]{1,3,2,0:T(8,128)(2,1)} copy(bf16[4,1024,3,64]{3,2,1,0:T(4,128)(2,1)} %reshape.289) | data formatting | bytes 3145728 | tf_op jit(solution)/shard_map/reshape | solution.py:42
  317.2 1.8 convolution_multiply_fusion
  319.0 1.7 fusion.42
  320.6 3.9 fusion.7
  324.5 3.8 copy.129
  328.4 5.4 reshape.244
  333.8 4.0 reshape.288
  337.8 5.6 copy.119
  343.4 1.6 fusion.43
  345.0 5.8 fusion.6
  350.8 3.8 copy.127
  354.5 5.4 reshape.243
  360.0 6.7 %pad_maximum_fusion = bf16[64,64,384]{1,0,2:T(8,128)(2,1)} fusion(bf16[64,64,192]{1,0,2:T(8,128)(2,1)} %reshape.244, bf16[64,64,192]{1,0,2:T(8,128)(2,1)} %reshape.243), kind=kLoop, calls=%fused_computation.7 | loop fusion | flops 1572864 | bytes 6291456 | tf_op jit(solution)/shard_map/concatenate | solution.py:81
  366.6 9.1 %copy.130 = bf16[64,64,384]{2,1,0:T(8,128)(2,1)} copy(bf16[64,64,384]{1,0,2:T(8,128)(2,1)} %pad_maximum_fusion) | data formatting | bytes 6291456 | tf_op jit(solution)/shard_map/concatenate | solution.py:81
  375.7 3.7 broadcast_in_dim.17
  379.4 11.8 %scatter_fusion.1 = bf16[64,2,64,384]{3,2,1,0:T(8,128)(2,1)} fusion(bf16[64,2,64,384]{3,2,1,0:T(8,128)(2,1)} %broadcast_in_dim.17, s32[64]{0:T(128)S(1)} %fusion.33, bf16[64,64,384]{2,1,0:T(8,128)(2,1)} %copy.130), kind=kCustom, calls=%fused_computation.3 | custom fusion | bytes 9437696 | tf_op jit(solution)/shard_map/scatter | solution.py:85
  391.2 10.7 %all-to-all-start.2 = ((bf16[64,2,64,384]{3,2,1,0:T(8,128)(2,1)}), bf16[64,2,64,384]{3,2,1,0:T(8,128)(2,1)}, u32[]{:S(2)}, u32[]{:S(2)}) async-start(bf16[64,2,64,384]{3,2,1,0:T(8,128)(2,1)} %scatter_fusion.1), calls=%async_computation.2 | async-start | bytes 12582912 | tf_op jit(solution)/shard_map/all_to_all | solution.py:87
  402.0 5.0 fusion.17
  407.2 0.2 convolution_convert_fusion.5
  407.4 0.6 copy.133
  408.0 1.1 reshape.279
  409.2 2.6 fusion.20
  412.0 0.2 convolution_convert_fusion.6
  412.3 0.6 copy.131
  412.8 1.1 reshape.277
  413.9 0.3 reduce-scatter.14.cloned.1.call-start
  414.2 128.5 %all-to-all-done.2 = bf16[64,2,64,384]{3,2,1,0:T(8,128)(2,1)} async-done(((bf16[64,2,64,384]{3,2,1,0:T(8,128)(2,1)}), bf16[64,2,64,384]{3,2,1,0:T(8,128)(2,1)}, u32[]{:S(2)}, u32[]{:S(2)}) %all-to-all-start.2) | async-done | bytes 6291488 | tf_op jit(solution)/shard_map/all_to_all | solution.py:87
  542.7 7.5 %copy.147 = bf16[16,8,64,384]{3,1,2,0:T(8,128)(2,1)S(1)} copy(bf16[16,8,64,384]{3,2,1,0:T(8,128)(2,1)} %bitcast.28) | data formatting | bytes 12582912
  550.2 0.9 convolution_convert_fusion
  551.3 0.9 copy-done.6
  552.2 0.2 copy-done.8
  552.4 1.6 convolution_convert_fusion.2
  554.0 5.7 copy.135
  559.7 7.4 %reshape.281 = bf16[1152,1024]{1,0:T(8,128)(2,1)} reshape(bf16[1152,16,64]{2,1,0:T(8,128)(2,1)} %bitcast.82) | data formatting | bytes 4718592
  567.1 0.9 reshape.280
  568.1 0.8 copy.134
  568.8 0.9 reshape.278
  569.8 0.8 copy.132
  570.6 27.3 %reduce-scatter.14.cloned.1.call-done = bf16[288,1024]{1,0:T(8,128)(2,1)} async-done(((bf16[1152,1024]{1,0:T(8,128)(2,1)}), bf16[288,1024]{1,0:T(8,128)(2,1)}) %reduce-scatter.14.cloned.1.call-update) | async-done | bytes 589840
  597.9 1.9 reshape.282
  599.7 1.6 copy.136
  (51 shorter events, 2.0 us)
Async XLA Ops:
  7.2 19.2 %copy-start = (bf16[16,64,1152]{2,1,0:T(8,128)(2,1)S(1)}, bf16[16,64,1152]{2,1,0:T(8,128)(2,1)}, u32[]{:S(2)}) copy-start(bf16[16,64,1152]{2,1,0:T(8,128)(2,1)} %param.8) | copy-start | bytes 7077892
  13.3 22.2 %all-to-all-start = ((s32[64,1,2]{2,1,0:T(1,128)}), s32[64,1,2]{2,1,0:T(1,128)S(1)}, u32[]{:S(2)}, u32[]{:S(2)}) async-start(s32[64,1,2]{2,1,0:T(1,128)} %copy.108), calls=%async_computation | async-start | bytes 65536 | tf_op jit(solution)/shard_map/all_to_all | solution.py:29
  26.3 264.8 %all-gather.2.cloned.1.call-start = ((), (), s32[]{:S(2)}) async-start(), calls=%async_computation.6 | async-start | bytes 11796480 | tf_op jit(solution)/shard_map/all_gather | solution.py:39
  199.7 1.0 copy-start.4
  199.7 1.0 copy-start.11
  199.7 1.6 copy-start.3
  199.8 1.6 copy-start.12
  199.8 2.1 copy-start.9
  200.8 1.4 copy-start.10
  202.2 97.2 %copy-start.5 = (bf16[1152,192]{1,0:T(8,128)(2,1)}, bf16[1152,192]{1,0:T(8,128)(2,1)S(1)}, u32[]{:S(2)}) copy-start(bf16[1152,192]{1,0:T(8,128)(2,1)S(1)} %copy.112) | copy-start | bytes 1327108
  202.4 96.9 %copy-start.7 = (bf16[1152,192]{1,0:T(8,128)(2,1)}, bf16[1152,192]{1,0:T(8,128)(2,1)S(1)}, u32[]{:S(2)}) copy-start(bf16[1152,192]{1,0:T(8,128)(2,1)S(1)} %copy.113) | copy-start | bytes 1327108
  319.0 1.7 copy-start.2
  391.2 151.6 %all-to-all-start.2 = ((bf16[64,2,64,384]{3,2,1,0:T(8,128)(2,1)}), bf16[64,2,64,384]{3,2,1,0:T(8,128)(2,1)}, u32[]{:S(2)}, u32[]{:S(2)}) async-start(bf16[64,2,64,384]{3,2,1,0:T(8,128)(2,1)} %scatter_fusion.1), calls=%async_computation.2 | async-start | bytes 12582912 | tf_op jit(solution)/shard_map/all_to_all | solution.py:87
  401.9 165.2 %reduce-scatter.12.cloned.1.call-start = ((), (), s32[]{:S(2)}) async-start(), calls=%async_computation.8 | async-start | bytes 245760
  409.1 159.7 %reduce-scatter.10.cloned.1.call-start = ((), (), s32[]{:S(2)}) async-start(), calls=%async_computation.7 | async-start | bytes 245760
  413.9 183.9 %reduce-scatter.14.cloned.1.call-start = ((), (), s32[]{:S(2)}) async-start(), calls=%async_computation.9 | async-start | bytes 2949120
  551.1 1.1 copy-start.6
  551.1 1.2 copy-start.8
  569.8 31.6 %copy-start.1 = (bf16[16,64,1152]{2,1,0:T(8,128)(2,1)S(1)}, bf16[16,64,1152]{2,1,0:T(8,128)(2,1)}, u32[]{:S(2)}) copy-start(bf16[16,64,1152]{2,1,0:T(8,128)(2,1)} %param.8) | copy-start | bytes 7077892
Sparse Core Ops, SparseCore 0:
  199.9 91.1 all-gather.1
  409.2 22.0 reduce-scatter.11
  434.0 23.0 reduce-scatter.9
  567.2 30.6 reduce-scatter.13
where the time goes:
time: 614 us; the launch traced here: 608 us
  waiting for transfers between devices  253 us (41%)
  blocking collectives  146 us (24%)
  local copies, waits for them, and re-layouts  126 us (21%)
  matrix products  32.2 us (5%)
  starting transfers between devices  24.1 us (4%)
  between operations  14.6 us (2%)
  other arithmetic  12.3 us (2%)
    all_to_all x1, blocking collectives, body(): lax.all_to_all(outgoing, 'frames', split_axis=0, concat_axis=0, tiled=True)  146 us
    all_to_all x1, waiting for transfers between devices, body(): lax.all_to_all(send_back, 'frames', split_axis=0, concat_axis=0, tiled=True)  128 us
    all_gather x1, waiting for transfers between devices, body(): lax.all_gather(chosen, 'mp', axis=1, tiled=True)  88.7 us
    unnamed x42, local copies, waits for them, and re-layouts  33.5 us
    unnamed x7, waiting for transfers between devices  27.4 us
    reshape x2, local copies, waits for them, and re-layouts, body(): both[:, :, :head_cols]  15.2 us
    all_to_all x1, starting transfers between devices, body(): lax.all_to_all(requests, 'frames', split_axis=0, concat_axis=0, tiled=True)  13 us
  transfers between devices with their start and end apart: 6, of which 4 were waited for; matrix products, arithmetic and copies ran while one was open for 7% of the time, Pallas kernels for 0%

commit v1 on v0

v1 whole, which is shorter than its diff:
```python
import functools

import jax
import jax.numpy as jnp
from jax import lax
from jax.experimental import pallas as pl
from jax.experimental.pallas import tpu as pltpu
from jax.sharding import PartitionSpec as P

HEAD_DIM = 64
NT = (((1,), (1,)), ((), ()))
TN = (((0,), (0,)), ((), ()))
NN = (((1,), (0,)), ((), ()))
F32 = jnp.float32
BF16 = jnp.bfloat16


def dot(a, b, dims):
    return lax.dot_general(a, b, dims, preferred_element_type=F32)


def head_masks(heads, wide):
    lane = lax.broadcasted_iota(jnp.int32, (1, wide), 1) // HEAD_DIM
    low = [(lane == h).astype(BF16) for h in range(heads)]
    high = [(lane == h + 1).astype(BF16) for h in range(heads)]
    return low, high


def spread(block, masks):
    return jnp.concatenate([block * m for m in masks], axis=0)


def gathered(block, masks, nq):
    total = block[:nq] * masks[0].astype(F32)
    for h in range(1, len(masks)):
        total = total + block[h * nq:(h + 1) * nq] * masks[h].astype(F32)
    return total


def pick_of(code, frames_here):
    code = jnp.maximum(code - 1, 0)
    return code // frames_here, code % frames_here


def products(x_ref, kv_ref, src, code, nq, tok, quests, frames_here, low, high):
    quest, local = pick_of(code, frames_here)
    rows = pl.multiple_of((src * quests + quest) * nq, nq)
    keys = pl.multiple_of(local * tok, tok)
    qm = spread(x_ref[pl.ds(rows, nq), 0:256], low)
    dm = spread(x_ref[pl.ds(rows, nq), 128:384], high)
    k = kv_ref[pl.ds(keys, tok), 0:256]
    v = kv_ref[pl.ds(keys, tok), 128:384]
    return dot(k, qm, NT), dot(v, dm, NT), qm, dm, k, v, keys


def stats_kernel(codes_ref, x_ref, kv_ref, out_ref, *, srcs, cap, nq, tok, quests, frames_here, heads):
    low, high = head_masks(heads, 256)

    def step(src, carry):
        @pl.when(codes_ref[src * cap] > 0)
        def _():
            for r in range(cap):
                s, dp, *_ = products(
                    x_ref, kv_ref, src, codes_ref[src * cap + r], nq, tok, quests, frames_here, low, high
                )
                m = jnp.max(s, axis=0, keepdims=True)
                e = jnp.exp(s - m)
                out_ref[src, 3 * r:3 * r + 1, 0:heads * nq] = m
                out_ref[src, 3 * r + 1:3 * r + 2, 0:heads * nq] = jnp.sum(e, axis=0, keepdims=True)
                out_ref[src, 3 * r + 2:3 * r + 3, 0:heads * nq] = jnp.sum(e * dp, axis=0, keepdims=True)

        return carry

    lax.fori_loop(0, srcs, step, 0)


def combine_kernel(quest_ref, st_ref, out_ref, *, cap, quests):
    ids = [quest_ref[r] for r in range(cap)]
    top = [st_ref[:, 3 * r, :] for r in range(cap)]
    size = [st_ref[:, 3 * r + 1, :] for r in range(cap)]
    mean = [st_ref[:, 3 * r + 2, :] for r in range(cap)]
    outs = [[jnp.zeros_like(top[0]) for _ in range(3)] for _ in range(cap)]
    for j in range(quests):
        on = [ids[r] == j for r in range(cap)]
        big = functools.reduce(
            jnp.maximum,
            [jnp.max(jnp.where(on[r], top[r], -jnp.inf), axis=0, keepdims=True) for r in range(cap)],
        )
        norm, delta = 0.0, 0.0
        for r in range(cap):
            e = jnp.exp(top[r] - big)
            norm = norm + jnp.sum(jnp.where(on[r], e * size[r], 0.0), axis=0, keepdims=True)
            delta = delta + jnp.sum(jnp.where(on[r], e * mean[r], 0.0), axis=0, keepdims=True)
        inv = 1.0 / norm
        for r in range(cap):
            for i, val in enumerate((big, inv, delta * inv)):
                outs[r][i] = jnp.where(on[r], val, outs[r][i])
    for r in range(cap):
        for i in range(3):
            out_ref[:, 3 * r + i, :] = outs[r][i]


def main_kernel(
    codes_ref, x_ref, kv_ref, st_ref, ret_ref, sum_ref, acc_ref, *, srcs, cap, nq, tok, quests, frames_here, heads, scale
):
    low, high = head_masks(heads, 256)
    acc_ref[...] = jnp.zeros_like(acc_ref)
    wide = heads * nq

    def step(src, carry):
        @pl.when(codes_ref[src * cap] > 0)
        def _():
            for r in range(cap):
                s, dp, qm, dm, k, v, keys = products(
                    x_ref, kv_ref, src, codes_ref[src * cap + r], nq, tok, quests, frames_here, low, high
                )
                m = st_ref[src, 3 * r:3 * r + 1, 0:wide]
                inv = st_ref[src, 3 * r + 1:3 * r + 2, 0:wide]
                delta = st_ref[src, 3 * r + 2:3 * r + 3, 0:wide]
                p = jnp.exp(s - m) * inv
                w = p.astype(BF16)
                ds = (p * (dp - delta)).astype(BF16)
                o = gathered(dot(w, v, TN), high, nq)
                dq = gathered(dot(ds, k, TN), low, nq) * scale
                dk = dot(ds, qm, NN)
                dv = dot(w, dm, NN)
                row = pl.multiple_of((src * cap + r) * nq, nq)
                ret_ref[pl.ds(row, nq), 0:128] = dq[:, 0:128].astype(BF16)
                ret_ref[pl.ds(row, nq), 128:256] = (dq[:, 128:256] + o[:, 0:128]).astype(BF16)
                ret_ref[pl.ds(row, nq), 256:384] = o[:, 128:256].astype(BF16)
                acc_ref[pl.ds(keys, tok), 0:128] += dk[:, 0:128]
                acc_ref[pl.ds(keys, tok), 128:256] += dk[:, 128:256] + dv[:, 0:128]
                acc_ref[pl.ds(keys, tok), 256:384] += dv[:, 128:256]

        @pl.when(codes_ref[src * cap] == 0)
        def _():
            row = pl.multiple_of(src * cap * nq, nq)
            ret_ref[pl.ds(row, cap * nq), :] = jnp.zeros((cap * nq, ret_ref.shape[1]), BF16)

        return carry

    lax.fori_loop(0, srcs, step, 0)
    sum_ref[...] = acc_ref[...].astype(BF16)


def collect_kernel(codes_ref, ret_ref, out_ref, acc_ref, *, slots, nq, frames_here):
    acc_ref[...] = jnp.zeros_like(acc_ref)

    def step(slot, carry):
        code = codes_ref[slot]

        @pl.when(code > 0)
        def _():
            quest, _ = pick_of(code, frames_here)
            to = pl.multiple_of(quest * nq, nq)
            at = pl.multiple_of(slot * nq, nq)
            acc_ref[pl.ds(to, nq), :] += ret_ref[pl.ds(at, nq), :].astype(F32)

        return carry

    lax.fori_loop(0, slots, step, 0)
    out_ref[...] = acc_ref[...].astype(BF16)


def call(kernel, out_shape, ins, scratch=()):
    spaces = {"s": pltpu.SMEM, "v": pltpu.VMEM}
    return pl.pallas_call(
        kernel,
        out_shape=out_shape,
        in_specs=[pl.BlockSpec(memory_space=spaces[i]) for i in ins],
        out_specs=jax.tree.map(lambda _: pl.BlockSpec(memory_space=pltpu.VMEM), out_shape),
        scratch_shapes=list(scratch),
        compiler_params=pltpu.CompilerParams(vmem_limit_bytes=40 * 1024 * 1024),
    )


def body(frames, keyframes, query_states, w_query, w_key, w_value, w_out, out_grad):
    owners = lax.axis_size("frames")
    shards = lax.axis_size("mp")
    fr_count, tok, width = frames.shape
    quests, keys = keyframes.shape
    nq = query_states.shape[1]
    hid = query_states.shape[2]
    cols = w_key.shape[1]
    heads = cols // HEAD_DIM
    scale = HEAD_DIM ** (-0.5)
    count = quests * keys
    cap = max(2, count // owners)

    picks = keyframes.reshape(-1)
    owner = picks // fr_count
    position = jnp.arange(count)
    same = owner[:, None] == owner[None, :]
    rank = jnp.sum(jnp.logical_and(same, position[None, :] < position[:, None]), axis=1)
    code = picks % fr_count + fr_count * (position // keys) + 1
    slot = owner * cap + rank
    requests = jnp.sum(
        jnp.where(slot[None, :] == jnp.arange(owners * cap)[:, None], code[None, :], 0), axis=1
    ).astype(jnp.int32)
    incoming = lax.all_to_all(
        requests.reshape(owners, cap), "frames", split_axis=0, concat_axis=0, tiled=True
    ).reshape(-1)
    quest_of = jnp.where(requests > 0, (requests - 1) // fr_count, -1).reshape(owners, cap)
    quest_of = jnp.broadcast_to(quest_of.T[:, :, None], (cap, owners, 128))

    queries = jnp.dot(query_states.reshape(quests * nq, hid), w_query, preferred_element_type=F32)
    d_mixed = lax.dot_general(out_grad.reshape(quests * nq, hid), w_out, NT, preferred_element_type=F32)
    local = jnp.concatenate([queries.astype(BF16) * scale, d_mixed.astype(BF16)], axis=1)
    everyone = lax.all_gather(local, "frames", axis=0, tiled=True)

    w_both = jnp.concatenate([w_key, w_value], axis=1)
    bank = jnp.dot(frames.reshape(fr_count * tok, width), w_both, preferred_element_type=F32).astype(BF16)
    w_mine = lax.all_to_all(
        jnp.concatenate(
            [w_query.reshape(shards, hid // shards, cols), w_out.reshape(cols, shards, hid // shards).swapaxes(0, 1)],
            axis=2,
        ),
        "mp",
        split_axis=0,
        concat_axis=0,
        tiled=True,
    )

    dims = dict(srcs=owners, cap=cap, nq=nq, tok=tok, quests=quests, frames_here=fr_count, heads=heads)
    stat_shape = jax.ShapeDtypeStruct((owners, 8, 128), F32)
    stats = call(functools.partial(stats_kernel, **dims), stat_shape, "svv")(incoming, everyone, bank)
    stats = lax.all_to_all(stats, "frames", split_axis=0, concat_axis=0, tiled=True)
    stats = call(functools.partial(combine_kernel, cap=cap, quests=quests), stat_shape, "vv")(quest_of, stats)
    stats = lax.all_to_all(stats, "frames", split_axis=0, concat_axis=0, tiled=True)
    partial, sums = call(
        functools.partial(main_kernel, scale=scale, **dims),
        (
            jax.ShapeDtypeStruct((owners * cap * nq, 2 * cols), BF16),
            jax.ShapeDtypeStruct((fr_count * tok, 2 * cols), BF16),
        ),
        "svvv",
        [pltpu.VMEM((fr_count * tok, 2 * cols), F32)],
    )(incoming, everyone, bank, stats)
    partial = lax.all_to_all(
        partial.reshape(owners, cap * nq, 2 * cols), "frames", split_axis=0, concat_axis=0, tiled=True
    ).reshape(owners * cap * nq, 2 * cols)

    grad_terms = lax.dot_general(w_both, sums, NT, preferred_element_type=F32).astype(BF16)
    frame_grad = lax.psum_scatter(grad_terms, "mp", scatter_dimension=0, tiled=True)
    frame_grad = frame_grad.T.reshape(fr_count, tok, width // shards)

    mine = call(
        functools.partial(collect_kernel, slots=owners * cap, nq=nq, frames_here=fr_count),
        jax.ShapeDtypeStruct((quests * nq, 2 * cols), BF16),
        "sv",
        [pltpu.VMEM((quests * nq, 2 * cols), F32)],
    )(requests, partial)
    full = lax.all_gather(mine, "mp", axis=0)
    query_grad = jnp.einsum("jrh,jch->rc", full[:, :, :cols], w_mine[:, :, :cols], preferred_element_type=F32)
    attended = jnp.einsum("jrh,jhc->rc", full[:, :, cols:], w_mine[:, :, cols:], preferred_element_type=F32)
    return (
        attended.astype(BF16).reshape(quests, nq, hid // shards),
        query_grad.astype(BF16).reshape(quests, nq, hid // shards),
        frame_grad,
    )


def solution(mesh):
    placed = (
        P("frames", None, None),
        P("frames", None),
        P("frames", None, None),
        P(None, "mp"),
        P(None, "mp"),
        P(None, "mp"),
        P("mp", None),
        P("frames", None, None),
    )
    return jax.shard_map(
        body,
        mesh=mesh,
        in_specs=placed,
        out_specs=(P("frames", None, "mp"), P("frames", None, "mp"), P("frames", None, "mp")),
        check_vma=False,
    )
```

time: 614 us -> 292 us (0.48)
  blocking collectives: 146 us -> 29.1 us
  waiting for transfers between devices: 253 us -> 141 us
  local copies, waits for them, and re-layouts: 126 us -> 21.6 us
  Pallas kernels: 0 us -> 32.9 us
  matrix products: 32.2 us -> 9.16 us
  starting transfers between devices: 24.1 us -> 40.8 us
  other arithmetic: 12.3 us -> 3.37 us
    all_to_all x1, blocking collectives: 146 us -> 17.8 us  [body(): lax.all_to_all(stats, 'frames', split_axis=0, concat_axis=0, tiled=True)]
    all_to_all x2 -> x4, waiting for transfers between devices: 137 us -> 80.7 us  [the longest x1 63.5 us: body(): lax.all_to_all(partial.reshape(owners, cap * nq, 2 * cols), 'frames', spl...]
    reshape x11 -> x4, local copies, waits for them, and re-layouts: 40.8 us -> 1.97 us  [the longest x1 1.1 us: body(): w_query.reshape(shards, hid // shards, cols)]
    pallas_call x0 -> x4, Pallas kernels: none -> 32.9 us  [the longest x1 20.4 us: body(): call(functools.partial(main_kernel, scale=scale, **dims), (jax.ShapeDtype...]
    all_gather x1, waiting for transfers between devices: 88.7 us -> 60.2 us  [body(): everyone = lax.all_gather(local, 'frames', axis=0, tiled=True)]
    unnamed x7 -> x2, waiting for transfers between devices: 27.4 us -> 0.03 us
    dot_general x13 -> x6, matrix products: 32.2 us -> 9.16 us  [the longest x1 4.09 us: body(): lax.dot_general(w_both, sums, NT, preferred_element_type=F32).astype(BF16)]
    unnamed x42 -> x23, local copies, waits for them, and re-layouts: 33.5 us -> 11.8 us
  transfers between devices with their start and end apart: 6 -> 6, of which waited for: 4 -> 4; matrix products, arithmetic and copies ran while one was open for 7% -> 6% of each run, Pallas kernels for 0% -> 1%
where the time goes in v1:
time: 292 us
  waiting for transfers between devices  141 us (48%)
  starting transfers between devices  40.8 us (14%)
  Pallas kernels  32.9 us (11%)
  blocking collectives  29.1 us (10%)
  local copies, waits for them, and re-layouts  21.6 us (7%)
  between operations  14.3 us (5%)
  matrix products  9.16 us (3%)
  other arithmetic  3.37 us (1%)
    all_to_all x1, waiting for transfers between devices, body(): lax.all_to_all(partial.reshape(owners, cap * nq, 2 * cols), 'frames', spl...  63.5 us
    all_gather x1, waiting for transfers between devices, body(): everyone = lax.all_gather(local, 'frames', axis=0, tiled=True)  60.2 us
    pallas_call x1, Pallas kernels, body(): call(functools.partial(main_kernel, scale=scale, **dims), (jax.ShapeDtype...  20.4 us
    all_to_all x1, blocking collectives, body(): lax.all_to_all(stats, 'frames', split_axis=0, concat_axis=0, tiled=True)  17.8 us
    all_to_all x1, starting transfers between devices, body(): lax.all_to_all(partial.reshape(owners, cap * nq, 2 * cols), 'frames', spl...  15.3 us
    all_to_all x1, starting transfers between devices, body(): lax.all_to_all(requests.reshape(owners, cap), 'frames', split_axis=0, con...  13 us
    unnamed x23, local copies, waits for them, and re-layouts  11.8 us
    all_to_all x1, waiting for transfers between devices, body(): lax.all_to_all(stats, 'frames', split_axis=0, concat_axis=0, tiled=True)  11.6 us
  transfers between devices with their start and end apart: 6, of which 4 were waited for; matrix products, arithmetic and copies ran while one was open for 6% of the time, Pallas kernels for 1%

profile of v1, /device:TPU:1, one launch (start us, length us, event | category | flops | bytes accessed | tf_op | source)
XLA Modules:
  0.0 292.3 jit_solution(11718370955764902527)
XLA Ops:
  7.2 0.0 copy-start
  7.2 0.0 copy-start.9
  7.2 0.0 all-gather.3.cloned.1.call-start
  7.2 1.5 convolution_convert_fusion.3
  8.7 0.1 copy.73
  8.8 1.3 convolution_convert_fusion.2
  10.2 0.1 copy.74
  10.3 0.7 pad_maximum_fusion.1
  11.0 0.0 all-gather.3.cloned.1.call-update
  11.0 0.8 reshape.160
  11.8 0.2 convert_reduce_fusion
  12.0 0.1 select_reduce_fusion.codes_ref
  12.1 0.8 all_to_all.18
  12.9 13.0 %all-to-all-start = ((s32[64,1,2]{2,1,0:T(1,128)}), s32[64,1,2]{2,1,0:T(1,128)S(1)}, u32[]{:S(2)}, u32[]{:S(2)}) async-start(s32[64,1,2]{2,1,0:T(1,128)} %bitcast), calls=%async_computation | async-start | bytes 65536 | tf_op jit(solution)/shard_map/all_to_all | solution.py:200
  25.9 1.1 constant_dynamic-update-slice_fusion.1
  26.9 0.0 copy-done.9
  27.0 0.0 copy-done
  27.0 0.0 copy-start.10
  27.0 1.0 copy-done.10
  28.0 1.5 fusion.kv_ref
  29.4 5.6 %all-to-all-done = s32[64,1,2]{2,1,0:T(1,128)S(1)} async-done(((s32[64,1,2]{2,1,0:T(1,128)}), s32[64,1,2]{2,1,0:T(1,128)S(1)}, u32[]{:S(2)}, u32[]{:S(2)}) %all-to-all-start) | async-done | bytes 544 | tf_op jit(solution)/shard_map/all_to_all | solution.py:200
  35.1 0.5 broadcast.190
  35.6 0.7 reduce.3
  36.3 0.1 reshape.161.codes_ref
  36.5 60.2 %all-gather.3.cloned.1.call-done.x_ref = bf16[8192,384]{1,0:T(8,128)(2,1)} async-done(((bf16[128,384]{1,0:T(8,128)(2,1)}), bf16[8192,384]{1,0:T(8,128)(2,1)}) %all-gather.3.cloned.1.call-update) | async-done | bytes 6291472 | tf_op jit(solution)/shard_map/all_gather | solution.py:209
  96.7 2.8 copy-done.1
  99.5 7.7 %shard_map.103 = f32[64,8,128]{2,1,0:T(8,128)S(1)} custom-call(s32[128]{0:T(128)S(1)} %reshape.161.codes_ref, bf16[8192,384]{1,0:T(8,128)(2,1)S(1)} %copy-done.1, bf16[1024,384]{1,0:T(8,128)(2,1)S(1)} %fusion.kv_ref), custom_call_target="tpu_custom_call" | custom-call | tf_op jit(solution)/shard_map/pallas_call | solution.py:226
  107.2 0.0 copy-start.4
  107.2 0.7 copy-done.4
  107.9 8.5 %all-to-all-start.1 = ((f32[64,8,128]{2,1,0:T(8,128)}), f32[64,8,128]{2,1,0:T(8,128)S(1)}, u32[]{:S(2)}, u32[]{:S(2)}) async-start(f32[64,8,128]{2,1,0:T(8,128)} %copy-done.4), calls=%async_computation.1 | async-start | bytes 524288 | tf_op jit(solution)/shard_map/all_to_all | solution.py:227
  116.4 0.1 sub.25
  116.5 0.2 gt.14
  116.7 0.1 copy.76
  116.8 11.6 %all-to-all-done.1.st_ref = f32[64,8,128]{2,1,0:T(8,128)S(1)} async-done(((f32[64,8,128]{2,1,0:T(8,128)}), f32[64,8,128]{2,1,0:T(8,128)S(1)}, u32[]{:S(2)}, u32[]{:S(2)}) %all-to-all-start.1) | async-done | bytes 262176 | tf_op jit(solution)/shard_map/all_to_all | solution.py:227
  128.4 0.1 broadcast_in_dim.18.quest_ref
  128.5 0.4 shard_map.104
  128.8 17.8 %all_to_all.29.st_ref = f32[64,8,128]{2,1,0:T(8,128)S(1)} all-to-all(f32[64,8,128]{2,1,0:T(8,128)S(1)} %shard_map.104), channel_id=1, replica_groups=mesh['frames'=64,'mp'=4] {'frames'}, dimensions={0} | all-to-all | bytes 524288 | tf_op jit(solution)/shard_map/all_to_all | solution.py:229
  146.7 2.8 copy-done.2
  149.5 20.4 %shard_map.105 = (bf16[4096,384]{1,0:T(8,128)(2,1)S(1)}, bf16[1024,384]{1,0:T(8,128)(2,1)S(1)}) custom-call(s32[128]{0:T(128)S(1)} %reshape.161.codes_ref, bf16[8192,384]{1,0:T(8,128)(2,1)S(1)} %copy-done.2, bf16[1024,384]{1,0:T(8,128)(2,1)S(1)} %fusion.kv_ref, f32[64,8,128]{2,1,0:T(8,128)S(1)} %all_to_all.29.st_ref), custom_call_target="tpu_custom_call" | custom-call | tf_op jit(solution)/shard_map/pallas_call | solution.py:230
  169.9 0.0 copy-start.3
  169.9 1.7 copy-done.3
  171.6 0.9 copy-done.5
  172.5 15.3 %all-to-all-start.3 = ((bf16[64,64,384]{2,1,0:T(8,128)(2,1)}), bf16[64,64,384]{2,1,0:T(8,128)(2,1)}, u32[]{:S(2)}, u32[]{:S(2)}) async-start(bf16[64,64,384]{2,1,0:T(8,128)(2,1)} %bitcast.35), calls=%async_computation.3 | async-start | bytes 6291456 | tf_op jit(solution)/shard_map/all_to_all | solution.py:239
  187.8 0.0 reduce-scatter.2.cloned.1.call-start
  187.8 0.0 copy-done.6
  187.8 4.1 %convolution_convert_fusion = bf16[1152,1024]{1,0:T(8,128)(2,1)} fusion(bf16[1152,384]{0,1:T(8,128)(2,1)} %copy-done.10, bf16[1024,384]{1,0:T(8,128)(2,1)S(1)} %copy-done.6), kind=kOutput, calls=%fused_computation | convolution fusion | flops 907149312 | bytes 4030464 | tf_op jit(solution)/shard_map/dot_general | solution.py:243
  191.9 0.0 reduce-scatter.2.cloned.1.call-update
  192.0 0.9 copy-done.7
  192.9 0.4 reshape.168
  193.2 0.0 copy-done.8
  193.3 1.1 reshape.167
  194.4 0.4 copy.78
  194.7 1.6 pad_maximum_fusion
  196.3 1.4 copy.79
  197.7 63.5 %all-to-all-done.3 = bf16[64,64,384]{2,1,0:T(8,128)(2,1)} async-done(((bf16[64,64,384]{2,1,0:T(8,128)(2,1)}), bf16[64,64,384]{2,1,0:T(8,128)(2,1)}, u32[]{:S(2)}, u32[]{:S(2)}) %all-to-all-start.3) | async-done | bytes 3145760 | tf_op jit(solution)/shard_map/all_to_all | solution.py:239
  261.2 4.0 %all-to-all-start.4 = ((bf16[4,192,384]{2,1,0:T(8,128)(2,1)}), bf16[4,192,384]{2,1,0:T(8,128)(2,1)S(1)}, u32[]{:S(2)}, u32[]{:S(2)}) async-start(bf16[4,192,384]{2,1,0:T(8,128)(2,1)} %copy.79), calls=%async_computation.4 | async-start | bytes 1179648 | tf_op jit(solution)/shard_map/all_to_all | solution.py:213
  265.2 2.2 copy.84
  267.4 4.4 %shard_map.106 = bf16[128,384]{1,0:T(8,128)(2,1)S(1)} custom-call(s32[128]{0:T(128)S(1)} %select_reduce_fusion.codes_ref, bf16[4096,384]{1,0:T(8,128)(2,1)} %bitcast.7.ret_ref), custom_call_target="tpu_custom_call" | custom-call | tf_op jit(solution)/shard_map/pallas_call | solution.py:247
  271.8 11.3 %all-gather = bf16[512,384]{1,0:T(8,128)(2,1)S(1)} all-gather(bf16[128,384]{1,0:T(8,128)(2,1)S(1)} %shard_map.106), channel_id=2, replica_groups=mesh['frames'=64,'mp'=4] {'mp'}, dimensions={0}, use_global_device_ids=true | all-gather | bytes 491520 | tf_op jit(solution)/shard_map/all_gather | solution.py:253
  283.1 0.0 all-to-all-done.4
  283.1 0.3 fusion.2
  283.4 0.7 copy.83
  284.2 0.6 fusion.1
  284.7 0.7 copy.81
  (14 shorter events, 0.1 us)
Async XLA Ops:
  7.2 19.8 %copy-start = (bf16[16,64,1152]{2,1,0:T(8,128)(2,1)S(1)}, bf16[16,64,1152]{2,1,0:T(8,128)(2,1)}, u32[]{:S(2)}) copy-start(bf16[16,64,1152]{2,1,0:T(8,128)(2,1)} %param.8) | copy-start | bytes 7077892
  7.2 19.7 %copy-start.9 = (bf16[1152,192]{0,1:T(8,128)(2,1)S(1)}, bf16[1152,192]{0,1:T(8,128)(2,1)}, u32[]{:S(2)}) copy-start(bf16[1152,192]{0,1:T(8,128)(2,1)} %param.13) | copy-start | bytes 1327108
  7.2 89.5 %all-gather.3.cloned.1.call-start = ((), (), s32[]{:S(2)}) async-start(), calls=%async_computation.6 | async-start | bytes 6389760 | tf_op jit(solution)/shard_map/all_gather | solution.py:209
  12.9 22.2 %all-to-all-start = ((s32[64,1,2]{2,1,0:T(1,128)}), s32[64,1,2]{2,1,0:T(1,128)S(1)}, u32[]{:S(2)}, u32[]{:S(2)}) async-start(s32[64,1,2]{2,1,0:T(1,128)} %bitcast), calls=%async_computation | async-start | bytes 65536 | tf_op jit(solution)/shard_map/all_to_all | solution.py:200
  27.0 1.0 copy-start.10
  96.7 2.8 copy-start.1
  107.2 0.7 copy-start.4
  107.9 20.5 %all-to-all-start.1 = ((f32[64,8,128]{2,1,0:T(8,128)}), f32[64,8,128]{2,1,0:T(8,128)S(1)}, u32[]{:S(2)}, u32[]{:S(2)}) async-start(f32[64,8,128]{2,1,0:T(8,128)} %copy-done.4), calls=%async_computation.1 | async-start | bytes 524288 | tf_op jit(solution)/shard_map/all_to_all | solution.py:227
  146.7 2.8 copy-start.2
  169.9 1.7 copy-start.3
  171.6 0.9 copy-start.5
  172.5 15.4 %copy-start.6 = (bf16[1024,384]{1,0:T(8,128)(2,1)S(1)}, bf16[1024,384]{1,0:T(8,128)(2,1)}, u32[]{:S(2)}) copy-start(bf16[1024,384]{1,0:T(8,128)(2,1)} %copy-done.5) | copy-start | bytes 2359300
  172.5 88.8 %all-to-all-start.3 = ((bf16[64,64,384]{2,1,0:T(8,128)(2,1)}), bf16[64,64,384]{2,1,0:T(8,128)(2,1)}, u32[]{:S(2)}, u32[]{:S(2)}) async-start(bf16[64,64,384]{2,1,0:T(8,128)(2,1)} %bitcast.35), calls=%async_computation.3 | async-start | bytes 6291456 | tf_op jit(solution)/shard_map/all_to_all | solution.py:239
  187.8 77.4 %reduce-scatter.2.cloned.1.call-start = ((), (), s32[]{:S(2)}) async-start(), calls=%async_computation.7 | async-start | bytes 2949120 | tf_op jit(solution)/shard_map/reduce_scatter | solution.py:244
  191.9 1.0 copy-start.7
  191.9 1.3 copy-start.8
  261.2 21.9 %all-to-all-start.4 = ((bf16[4,192,384]{2,1,0:T(8,128)(2,1)}), bf16[4,192,384]{2,1,0:T(8,128)(2,1)S(1)}, u32[]{:S(2)}, u32[]{:S(2)}) async-start(bf16[4,192,384]{2,1,0:T(8,128)(2,1)} %copy.79), calls=%async_computation.4 | async-start | bytes 1179648 | tf_op jit(solution)/shard_map/all_to_all | solution.py:213
Sparse Core Ops, SparseCore 0:
  11.3 85.2 all-gather.2
  192.1 35.3 reduce-scatter.1

commit v2 on v1

v2 whole, which is shorter than its diff:
```python
import functools

import jax
import jax.numpy as jnp
from jax import lax
from jax.experimental import pallas as pl
from jax.experimental.pallas import tpu as pltpu
from jax.sharding import PartitionSpec as P

HEAD_DIM = 64
NT = (((1,), (1,)), ((), ()))
TN = (((0,), (0,)), ((), ()))
NN = (((1,), (0,)), ((), ()))
F32 = jnp.float32
BF16 = jnp.bfloat16


def dot(a, b, dims):
    return lax.dot_general(a, b, dims, preferred_element_type=F32)


def head_masks(heads, wide):
    lane = lax.broadcasted_iota(jnp.int32, (1, wide), 1) // HEAD_DIM
    low = [(lane == h).astype(BF16) for h in range(heads)]
    high = [(lane == h + 1).astype(BF16) for h in range(heads)]
    return low, high


def spread(block, masks):
    return jnp.concatenate([block * m for m in masks], axis=0)


def gathered(block, masks, nq):
    total = block[:nq] * masks[0].astype(F32)
    for h in range(1, len(masks)):
        total = total + block[h * nq:(h + 1) * nq] * masks[h].astype(F32)
    return total


AXES = (4, 8, 2)
FIRST = 3


def frames_perm(dx=0, dz=0, dc=0):
    nx, nz, nc = AXES
    pairs = []
    for x in range(nx):
        for z in range(nz):
            for c in range(nc):
                to = (((x + dx) % nx) * nz + (z + dz) % nz) * nc + (c + dc) % nc
                pairs.append(((x * nz + z) * nc + c, to))
    return pairs


def planes():
    nx, nz, nc = AXES
    number = lambda x, z, c: (x * nz + z) * nc + c
    flat = [[number(x, z, c) for x in range(nx) for c in range(nc)] for z in range(nz)]
    line = [[number(x, z, c) for z in range(nz)] for x in range(nx) for c in range(nc)]
    return flat, line


def hop(value, **shift):
    return lax.ppermute(value, "frames", frames_perm(**shift))


def plan_kernel(codes_ref, me_ref, order_ref, size_ref, at_ref, *, cap, quests, nq, tok, frames_here):
    nx, nz, nc = AXES
    owners = nx * nz * nc
    bits = frames_here.bit_length() - 1
    me = me_ref[0]
    x, z, c = lax.div(me, nz * nc), lax.rem(lax.div(me, nc), nz), lax.rem(me, nc)

    def step(block, found):
        at, core, across = lax.div(block, nc * nx), lax.rem(lax.div(block, nx), nc), lax.rem(block, nx)
        away = jnp.where(lax.rem(at, 2) == 1, lax.div(at + 1, 2), nz - lax.div(at, 2))
        there = lax.rem(x - across + nx, nx) * nz + lax.rem(z - away + nz, nz)
        src = there * nc + lax.rem(c + core, nc)
        asks = (lax.rem(there, nz) * nx + lax.div(there, nz)) * nc + lax.rem(c + core, nc)
        valid = codes_ref[asks * cap] > 0
        order_ref[jnp.where(valid, found, owners - 1 - (block - found))] = src
        for r in range(cap):
            code = jnp.maximum(codes_ref[asks * cap + r] - 1, 0)
            row = (block * quests + (code >> bits)) * nq
            at_ref[src * cap + r] = jnp.where(valid, row, 0)
            at_ref[(owners + src) * cap + r] = (code & (frames_here - 1)) * tok
        return found + jnp.where(valid, 1, 0)

    near = lax.fori_loop(0, FIRST * nx * nc, step, 0)
    size_ref[1] = near
    size_ref[0] = lax.fori_loop(FIRST * nx * nc, owners, step, near)


def load_rows(pieces, x_ref, sems):
    copies, row = [], 0
    full = pieces[0].shape[0]
    for i, piece in enumerate(pieces):
        size = piece.shape[0]
        if size == full:
            row = i * full
        else:
            half, core = divmod(i - (len(pieces) - 4), 2)
            row = (len(pieces) - 4 + core) * full + half * size
        copies.append(pltpu.make_async_copy(piece, x_ref.at[pl.ds(row, size)], sems.at[i]))
        copies[-1].start()
    return copies


def in_groups(order_ref, size_ref, copies, group, step):
    early = size_ref[1] // group
    for c in copies[:2 * FIRST]:
        c.wait()
    lax.fori_loop(0, early, step, 0)
    for c in copies[2 * FIRST:]:
        c.wait()
    last = (size_ref[0] + group - 1) // group
    lax.fori_loop(early, last, step, 0)
    return last


def group_of(i, group, cap, order_ref):
    srcs = [order_ref[i * group + g] for g in range(group)]
    return srcs, [src * cap + r for src in srcs for r in range(cap)]


def rows_of(at_ref, slots, x_ref, kv_ref, nq, tok, low, high):
    at = [pl.multiple_of(at_ref[slot], nq) for slot in slots]
    keys = [pl.multiple_of(at_ref[at_ref.shape[0] // 2 + slot], tok) for slot in slots]
    qm = [spread(x_ref[pl.ds(a, nq), 0:256], low) for a in at]
    dm = [spread(x_ref[pl.ds(a, nq), 128:384], high) for a in at]
    k = [kv_ref[pl.ds(a, tok), 0:256] for a in keys]
    v = [kv_ref[pl.ds(a, tok), 128:384] for a in keys]
    s = [dot(a, b, NT) for a, b in zip(k, qm)]
    dp = [dot(a, b, NT) for a, b in zip(v, dm)]
    return s, dp, qm, dm, k, v, keys


def stats_kernel(order_ref, size_ref, at_ref, kv_ref, *refs, cap, nq, tok, heads, group):
    *pieces, out_ref, x_ref, sems = refs
    low, high = head_masks(heads, 256)
    copies = load_rows(pieces, x_ref, sems)
    wide = heads * nq

    def step(i, carry):
        srcs, slots = group_of(i, group, cap, order_ref)
        s, dp, *_ = rows_of(at_ref, slots, x_ref, kv_ref, nq, tok, low, high)
        m = [jnp.max(a, axis=0, keepdims=True) for a in s]
        e = [jnp.exp(a - b) for a, b in zip(s, m)]
        for n, (a, b, c) in enumerate(zip(m, e, dp)):
            src, r = srcs[n // cap], 3 * (n % cap)
            out_ref[src, r:r + 1, 0:wide] = a
            out_ref[src, r + 1:r + 2, 0:wide] = jnp.sum(b, axis=0, keepdims=True)
            out_ref[src, r + 2:r + 3, 0:wide] = jnp.sum(b * c, axis=0, keepdims=True)
        return carry

    in_groups(order_ref, size_ref, copies, group, step)


def combine_kernel(quest_ref, st_ref, out_ref, *, cap, quests):
    ids = [quest_ref[r] for r in range(cap)]
    top = [st_ref[:, 3 * r, :] for r in range(cap)]
    size = [st_ref[:, 3 * r + 1, :] for r in range(cap)]
    mean = [st_ref[:, 3 * r + 2, :] for r in range(cap)]
    none = jnp.zeros_like(top[0])
    outs = [[none + 3e38, none, none] for _ in range(cap)]
    for j in range(quests):
        on = [ids[r] == j for r in range(cap)]
        big = functools.reduce(
            jnp.maximum,
            [jnp.max(jnp.where(on[r], top[r], -jnp.inf), axis=0, keepdims=True) for r in range(cap)],
        )
        norm, delta = 0.0, 0.0
        for r in range(cap):
            e = jnp.exp(top[r] - big)
            norm = norm + jnp.sum(jnp.where(on[r], e * size[r], 0.0), axis=0, keepdims=True)
            delta = delta + jnp.sum(jnp.where(on[r], e * mean[r], 0.0), axis=0, keepdims=True)
        inv = 1.0 / norm
        for r in range(cap):
            for i, val in enumerate((big, inv, delta * inv)):
                outs[r][i] = jnp.where(on[r], val, outs[r][i])
    for r in range(cap):
        for i in range(3):
            out_ref[:, 3 * r + i, :] = outs[r][i]


def main_kernel(
    order_ref, size_ref, at_ref, kv_ref, st_ref, x_ref, ret_ref, sum_ref, acc_ref, held_ref, sent,
    *, cap, nq, tok, heads, group, scale
):
    low, high = head_masks(heads, 256)
    acc_ref[...] = jnp.zeros_like(acc_ref)
    wide = heads * nq
    size = cap * nq

    def send(src):
        at = pl.ds(pl.multiple_of(src * size, size), size)
        pltpu.make_async_copy(held_ref.at[at], ret_ref.at[at], sent).start()

    def step(i, carry):
        srcs, slots = group_of(i, group, cap, order_ref)
        s, dp, qm, dm, k, v, keys = rows_of(at_ref, slots, x_ref, kv_ref, nq, tok, low, high)
        st = [
            [st_ref[src, 3 * r + n:3 * r + n + 1, 0:wide] for n in range(3)] for src in srcs for r in range(cap)
        ]
        p = [jnp.exp(a - b[0]) * b[1] for a, b in zip(s, st)]
        w = [a.astype(BF16) for a in p]
        ds = [(a * (b - c[2])).astype(BF16) for a, b, c in zip(p, dp, st)]
        o = [gathered(dot(a, b, TN), high, nq) for a, b in zip(w, v)]
        dq = [gathered(dot(a, b, TN), low, nq) * scale for a, b in zip(ds, k)]
        dk = [dot(a, b, NN) for a, b in zip(ds, qm)]
        dv = [dot(a, b, NN) for a, b in zip(w, dm)]
        for n, slot in enumerate(slots):
            row = pl.ds(pl.multiple_of(slot * nq, nq), nq)
            held_ref[row, 0:128] = dq[n][:, 0:128].astype(BF16)
            held_ref[row, 128:256] = (dq[n][:, 128:256] + o[n][:, 0:128]).astype(BF16)
            held_ref[row, 256:384] = o[n][:, 128:256].astype(BF16)
            at = pl.ds(keys[n], tok)
            acc_ref[at, 0:128] += dk[n][:, 0:128]
            acc_ref[at, 128:256] += dk[n][:, 128:256] + dv[n][:, 0:128]
            acc_ref[at, 256:384] += dv[n][:, 128:256]
        for src in srcs:
            send(src)
        return carry

    last = (size_ref[0] + group - 1) // group
    lax.fori_loop(0, last, step, 0)

    def rest(i, carry):
        src = order_ref[i]
        held_ref[pl.ds(pl.multiple_of(src * size, size), size), :] = jnp.zeros((size, held_ref.shape[1]), BF16)
        send(src)
        return carry

    lax.fori_loop(last * group, order_ref.shape[0], rest, 0)
    sum_ref[...] = acc_ref[...].astype(BF16)
    pltpu.make_async_copy(held_ref, ret_ref, sent).wait()


def finish_kernel(*refs, cols):
    *ins, att_ref, grad_ref = refs
    many = len(ins) // 2
    lane = lax.broadcasted_iota(jnp.int32, (1, 256), 1)
    low = (lane < cols).astype(BF16)
    high = (lane >= cols - 128).astype(BF16)
    att, grad = 0.0, 0.0
    for x_ref, w_ref in zip(ins[:many], ins[many:]):
        grad = grad + dot(x_ref[:, 0:256] * low, w_ref[:, 0:256], NT)
        att = att + dot(x_ref[:, 128:384] * high, w_ref[:, 128:384], NT)
    att_ref[...] = att.astype(BF16)
    grad_ref[...] = grad.astype(BF16)


def call(kernel, out_shape, ins, outs, scratch=(), mib=1):
    spaces = {"s": pltpu.SMEM, "v": pltpu.VMEM, "a": pltpu.HBM}
    out_specs = [pl.BlockSpec(memory_space=spaces[i]) for i in outs]
    return pl.pallas_call(
        kernel,
        out_shape=out_shape,
        in_specs=[pl.BlockSpec(memory_space=spaces[i]) for i in ins],
        out_specs=out_specs if len(outs) > 1 else out_specs[0],
        scratch_shapes=list(scratch),
        compiler_params=pltpu.CompilerParams(vmem_limit_bytes=mib * 1024 * 1024),
    )


def mp_hop(value, s):
    many = lax.axis_size("mp")
    return lax.ppermute(value, "mp", [(i, (i + s) % many) for i in range(many)])


def body(frames, keyframes, query_states, w_query, w_key, w_value, w_out, out_grad):
    owners = lax.axis_size("frames")
    shards = lax.axis_size("mp")
    me, shard = lax.axis_index("frames"), lax.axis_index("mp")
    fr_count, tok, width = frames.shape
    quests, keys = keyframes.shape
    nq = query_states.shape[1]
    hid = query_states.shape[2]
    cols = w_key.shape[1]
    heads = cols // HEAD_DIM
    scale = HEAD_DIM ** (-0.5)
    count = quests * keys
    cap = max(2, count // owners)
    group = 4

    queries = jnp.dot(query_states.reshape(quests * nq, hid), w_query, preferred_element_type=F32)
    d_mixed = lax.dot_general(out_grad.reshape(quests * nq, hid), w_out, NT, preferred_element_type=F32)
    local = jnp.concatenate([queries.astype(BF16) * scale, d_mixed.astype(BF16)], axis=1)
    picks = keyframes.reshape(-1)
    owner = picks >> (fr_count.bit_length() - 1)
    position = jnp.arange(count)
    same = owner[:, None] == owner[None, :]
    rank = jnp.sum(jnp.logical_and(same, position[None, :] < position[:, None]), axis=1)
    code = (picks & (fr_count - 1)) + fr_count * (position // keys) + 1
    slot = owner * cap + rank
    requests = jnp.sum(
        jnp.where(slot[None, :] == jnp.arange(owners * cap)[:, None], code[None, :], 0), axis=1
    ).astype(jnp.int32)
    asked = jnp.where(requests > 0, (requests - 1) >> (fr_count.bit_length() - 1), -1)
    quest_of = jnp.broadcast_to(asked.reshape(owners, cap).T[:, :, None], (cap, owners, 128))
    put = jnp.arange(quests * nq)[:, None]
    take = jnp.arange(owners * cap * nq)[None, :]
    pick_sum = jnp.logical_and(put // nq == jnp.repeat(asked, nq)[None, :], put % nq == take % nq).astype(BF16)

    w_both = jnp.concatenate([w_key, w_value], axis=1)
    bank = jnp.dot(frames.reshape(fr_count * tok, width), w_both, preferred_element_type=F32).astype(BF16)
    flat, line = planes()
    nx, nz, nc = AXES
    mine = jnp.concatenate([local] + [hop(local, dx=s) for s in range(1, nx)], axis=0)
    passed = requests.reshape(nx, nz, nc, cap).swapaxes(0, 1).reshape(nz, nx * nc * cap)
    passed = lax.all_to_all(passed, "frames", 0, 0, axis_index_groups=line, tiled=True)
    mine, passed, bank = lax.optimization_barrier((mine, passed, bank))
    incoming = passed.reshape(nz, nx * nc, cap).swapaxes(0, 1).reshape(nx * nc, nz * cap)
    incoming = lax.all_to_all(incoming, "frames", 0, 0, axis_index_groups=flat, tiled=True)
    incoming = incoming.reshape(nx * nc, nz, cap).swapaxes(0, 1).reshape(-1)
    ways = [(mine, mine)]
    ways.append((hop(ways[-1][0], dz=1), hop(ways[-1][1], dz=-1)))
    ways[-1], incoming = lax.optimization_barrier((ways[-1], incoming))
    ints = lambda *shape: jax.ShapeDtypeStruct(shape, jnp.int32)
    order, sizes, at = call(
        functools.partial(plan_kernel, cap=cap, quests=quests, nq=nq, tok=tok, frames_here=fr_count),
        (ints(owners), ints(2), ints(2 * owners * cap)),
        "ss",
        "sss",
    )(incoming, me.astype(jnp.int32).reshape(1))
    ways.append((hop(ways[-1][0], dz=1), hop(ways[-1][1], dz=-1)))
    ways[-1], order, sizes, at, quest_of = lax.optimization_barrier((ways[-1], order, sizes, at, quest_of))
    ways.append((hop(ways[-1][0], dz=1), hop(ways[-1][1], dz=-1)))
    half = mine.shape[0] // 2
    pieces = [mine] + [way for pair in ways[1:] for way in pair]
    pieces += [hop(ways[-1][0][:half], dz=1), hop(ways[-1][1][half:], dz=-1)]
    pieces = [p for piece in pieces for p in (piece, hop(piece, dc=1))]

    dims = dict(cap=cap, nq=nq, tok=tok, heads=heads, group=group)
    held = (owners * cap * nq, 2 * cols)
    stat_shape = jax.ShapeDtypeStruct((owners, 8, 128), F32)
    rows = jax.ShapeDtypeStruct((owners * quests * nq, 2 * cols), BF16)
    stats, rows = call(
        functools.partial(stats_kernel, **dims),
        (stat_shape, rows),
        "sssv" + "a" * len(pieces),
        "vv",
        [pltpu.SemaphoreType.DMA((len(pieces),))],
        4,
    )(order, sizes, at, bank, *pieces)
    stats = lax.all_to_all(stats, "frames", split_axis=0, concat_axis=0, tiled=True)
    stats = call(functools.partial(combine_kernel, cap=cap, quests=quests), stat_shape, "vv", "v")(quest_of, stats)
    stats = lax.all_to_all(stats, "frames", split_axis=0, concat_axis=0, tiled=True)
    partial, sums = call(
        functools.partial(main_kernel, scale=scale, **dims),
        (jax.ShapeDtypeStruct(held, BF16), jax.ShapeDtypeStruct((fr_count * tok, 2 * cols), BF16)),
        "sssvvv",
        "av",
        [
            pltpu.VMEM((fr_count * tok, 2 * cols), F32),
            pltpu.VMEM(held, BF16),
            pltpu.SemaphoreType.DMA(()),
        ],
        10,
    )(order, sizes, at, bank, stats, rows)
    partial = lax.all_to_all(
        partial.reshape(owners, cap * nq, 2 * cols), "frames", split_axis=0, concat_axis=0, tiled=True
    ).reshape(held)

    w_q_out = jnp.concatenate([w_query, w_out.T], axis=1)
    own = [(shard + s) % shards for s in range(shards)]
    part = hid // shards
    w_mine = [lax.dynamic_slice_in_dim(w_q_out, own[s] * part, part, 0) for s in range(shards)]
    w_mine = [w_mine[0]] + [mp_hop(w_mine[s], s) for s in range(1, shards)]
    slab = width // shards
    terms = [
        lax.dot_general(
            sums, lax.dynamic_slice_in_dim(w_both, own[s] * slab, slab, 0), NT, preferred_element_type=F32
        )
        for s in range(shards)
    ]
    frame_grad = terms[0]
    for s in range(1, shards):
        frame_grad = frame_grad + mp_hop(terms[s].astype(BF16), s).astype(F32)

    frame_grad = frame_grad.astype(BF16).reshape(fr_count, tok, slab)
    tied = (partial, frame_grad, w_mine, pick_sum)
    partial, frame_grad, w_mine, pick_sum = lax.optimization_barrier(tied)
    mine = jnp.dot(pick_sum, partial, preferred_element_type=F32).astype(BF16)
    full = [mine] + [mp_hop(mine, s) for s in range(1, shards)]
    out = jax.ShapeDtypeStruct((quests * nq, part), BF16)
    attended, query_grad = call(
        functools.partial(finish_kernel, cols=cols), (out, out), "v" * 2 * shards, "vv", mib=4
    )(*full, *w_mine)
    return (
        attended.reshape(quests, nq, part),
        query_grad.reshape(quests, nq, part),
        frame_grad,
    )


def solution(mesh):
    placed = (
        P("frames", None, None),
        P("frames", None),
        P("frames", None, None),
        P(None, "mp"),
        P(None, "mp"),
        P(None, "mp"),
        P("mp", None),
        P("frames", None, None),
    )
    return jax.shard_map(
        body,
        mesh=mesh,
        in_specs=placed,
        out_specs=(P("frames", None, "mp"), P("frames", None, "mp"), P("frames", None, "mp")),
        check_vma=False,
    )
```

time: 292 us -> 231 us (0.79)
  waiting for transfers between devices: 141 us -> 71.1 us
  blocking collectives: 29.1 us -> 48.5 us
  between operations: 14.3 us -> 1.14 us
  starting transfers between devices: 40.8 us -> 52.3 us
  Pallas kernels: 32.9 us -> 23.6 us
  local copies, waits for them, and re-layouts: 21.6 us -> 13.6 us
  matrix products: 9.16 us -> 12.5 us
  other arithmetic: 3.37 us -> 6.37 us
    all_gather x1 -> x0, waiting for transfers between devices: 60.2 us -> none  [body(): everyone = lax.all_gather(local, 'frames', axis=0, tiled=True)]
    ppermute x0 -> x29, waiting for transfers between devices: none -> 41.8 us  [the longest x9 28.3 us: mp_hop(): return lax.ppermute(value, 'mp', [(i, (i + s) % many) for i in range(many)])]
    all_to_all x1, waiting for transfers between devices: 63.5 us -> 26.2 us  [body(): lax.all_to_all(partial.reshape(owners, cap * nq, 2 * cols), 'frames', spl...]
    ppermute x0 -> x29, starting transfers between devices: none -> 36.2 us  [the longest x20 22.7 us: hop(): return lax.ppermute(value, 'frames', frames_perm(**shift))]
    all_to_all x1 -> x2, blocking collectives: 17.8 us -> 37 us  [body(): lax.all_to_all(stats, 'frames', split_axis=0, concat_axis=0, tiled=True)]
    all_to_all x3 -> x1, starting transfers between devices: 25.5 us -> 8.18 us  [body(): lax.all_to_all(passed, 'frames', 0, 0, axis_index_groups=line, tiled=True)]
    all_to_all x3 -> x1, waiting for transfers between devices: 17.2 us -> 3.1 us  [body(): lax.all_to_all(passed, 'frames', 0, 0, axis_index_groups=line, tiled=True)]
    all_to_all x0 -> x1, blocking collectives: none -> 11.5 us  [body(): lax.all_to_all(incoming, 'frames', 0, 0, axis_index_groups=flat, tiled=True)]
  transfers between devices with their start and end apart: 6 -> 31, of which waited for: 4 -> 13; matrix products, arithmetic and copies ran while one was open for 6% -> 10% of each run, Pallas kernels for 1% -> 2%
where the time goes in v2:
time: 231 us; the launch traced here: 229 us
  waiting for transfers between devices  71.1 us (31%)
  starting transfers between devices  52.3 us (23%)
  blocking collectives  48.5 us (21%)
  Pallas kernels  23.6 us (10%)
  local copies, waits for them, and re-layouts  13.6 us (6%)
  matrix products  12.5 us (5%)
  other arithmetic  6.37 us (3%)
    all_to_all x2, blocking collectives, body(): lax.all_to_all(stats, 'frames', split_axis=0, concat_axis=0, tiled=True)  37 us
    ppermute x9, waiting for transfers between devices, mp_hop(): return lax.ppermute(value, 'mp', [(i, (i + s) % many) for i in range(many)])  28.3 us
    all_to_all x1, waiting for transfers between devices, body(): lax.all_to_all(partial.reshape(owners, cap * nq, 2 * cols), 'frames', spl...  26.2 us
    ppermute x20, starting transfers between devices, hop(): return lax.ppermute(value, 'frames', frames_perm(**shift))  22.7 us
    ppermute x20, waiting for transfers between devices, hop(): return lax.ppermute(value, 'frames', frames_perm(**shift))  13.5 us
    ppermute x9, starting transfers between devices, mp_hop(): return lax.ppermute(value, 'mp', [(i, (i + s) % many) for i in range(many)])  13.5 us
    all_to_all x1, blocking collectives, body(): lax.all_to_all(incoming, 'frames', 0, 0, axis_index_groups=flat, tiled=True)  11.5 us
    pallas_call x1, Pallas kernels, body(): call(functools.partial(main_kernel, scale=scale, **dims), (jax.ShapeDtype...  10.9 us
  transfers between devices with their start and end apart: 31, of which 13 were waited for; matrix products, arithmetic and copies ran while one was open for 10% of the time, Pallas kernels for 2%

profile of v2, /device:TPU:1, one launch (start us, length us, event | category | flops | bytes accessed | tf_op | source)
XLA Modules:
  0.0 229.2 jit_solution(13260323005926220646)
XLA Ops:
  0.7 1.4 convolution_convert_fusion.5
  2.2 1.3 convolution_convert_fusion.6
  3.7 0.6 copy-done.9
  4.4 3.4 %collective-permute-start.2 = (bf16[128,384]{1,0:T(8,128)(2,1)S(1)}, bf16[128,384]{1,0:T(8,128)(2,1)S(1)}, u32[]{:S(2)}, u32[]{:S(2)}) collective-permute-start(bf16[128,384]{1,0:T(8,128)(2,1)S(1)} %pad_maximum_fusion.1), channel_id=1, source_target_pairs={{0,192},{4,196},{8,200},{12,204},{16,208},{20,212},{24,216},{28,22... | collective-permute-start | bytes 294920 | tf_op jit(solution)/shard_map/ppermute | solution.py:64
  7.8 0.5 collective-permute-start.1
  8.3 0.6 collective-permute-start
  8.9 0.7 broadcast_shift-right-arithmetic_fusion
  10.7 0.7 copy.66
  11.4 8.2 %all-to-all-start = ((s32[8,1,16]{2,1,0:T(1,128)}), s32[8,1,16]{2,1,0:T(1,128)S(1)}, u32[]{:S(2)}, u32[]{:S(2)}) async-start(s32[8,1,16]{2,1,0:T(1,128)} %copy.66), calls=%async_computation | async-start | bytes 8192 | tf_op jit(solution)/shard_map/all_to_all | solution.py:311
  19.7 1.5 fusion.3.kv_ref
  21.3 0.7 copy-done.13
  21.9 1.1 pad_maximum_fusion.refs_0_
  23.0 3.1 %all-to-all-done = s32[8,1,16]{2,1,0:T(1,128)S(1)} async-done(((s32[8,1,16]{2,1,0:T(1,128)}), s32[8,1,16]{2,1,0:T(1,128)S(1)}, u32[]{:S(2)}, u32[]{:S(2)}) %all-to-all-start) | async-done | bytes 544 | tf_op jit(solution)/shard_map/all_to_all | solution.py:311
  26.4 2.4 %collective-permute-start.4 = (bf16[512,384]{1,0:T(8,128)(2,1)S(1)}, bf16[512,384]{1,0:T(8,128)(2,1)}, u32[]{:S(2)}, u32[]{:S(2)}) collective-permute-start(bf16[512,384]{1,0:T(8,128)(2,1)S(1)} %pad_maximum_fusion.refs_0_), channel_id=1, source_target_pairs={{0,56},{4,60},{8,0},{12,4},{16,8},{20,12},{24,16},{28,20},{32,24},... | collective-permute-start | bytes 1179656 | tf_op jit(solution)/shard_map/ppermute | solution.py:64
  29.0 11.5 %all_to_all.36 = s32[8,1,16]{2,1,0:T(1,128)S(1)} all-to-all(s32[8,1,16]{2,1,0:T(1,128)S(1)} %copy.70), channel_id=1, replica_groups={{0,4,64,68,128,132,192,196},{8,12,72,76,136,140,200,204},{16,20,80,84,1..., dimensions={0} | all-to-all | bytes 1024 | tf_op jit(solution)/shard_map/all_to_all | solution.py:314
  40.6 0.7 copy.72
  41.3 0.9 reshape.182.codes_ref
  42.3 2.7 %collective-permute-start.6 = (bf16[512,384]{1,0:T(8,128)(2,1)}, bf16[512,384]{1,0:T(8,128)(2,1)}, u32[]{:S(2)}, u32[]{:S(2)}) collective-permute-start(bf16[512,384]{1,0:T(8,128)(2,1)} %collective-permute-done.4.refs_4_), channel_id=1, source_target_pairs={{0,56},{4,60},{8,0},{12,4},{16,8},{20,12},{24,16},{28,20},{32,24},... | collective-permute-start | bytes 1179656 | tf_op jit(solution)/shard_map/ppermute | solution.py:64
  45.0 0.6 compare_select_fusion
  45.6 0.8 select_n.99
  46.3 0.8 copy.73
  47.2 3.6 %shard_map.103 = (s32[64]{0:T(128)S(1)}, s32[2]{0:T(128)S(1)}, s32[256]{0:T(256)S(1)}) custom-call(s32[128]{0:T(128)S(1)} %reshape.182.codes_ref, s32[1]{0:T(128)} %bitcast.12.me_ref), custom_call_target="tpu_custom_call" | custom-call | tf_op jit(solution)/shard_map/pallas_call | solution.py:320
  50.8 3.0 %collective-permute-done.5.refs_6_ = bf16[512,384]{1,0:T(8,128)(2,1)} collective-permute-done((bf16[512,384]{1,0:T(8,128)(2,1)}, bf16[512,384]{1,0:T(8,128)(2,1)}, u32[]{:S(2)}, u32[]{:S(2)}) %collective-permute-start.5) | collective-permute-done | bytes 393248 | tf_op jit(solution)/shard_map/ppermute | solution.py:64
  53.9 2.7 %collective-permute-start.14 = (bf16[512,384]{1,0:T(8,128)(2,1)}, bf16[512,384]{1,0:T(8,128)(2,1)S(1)}, u32[]{:S(2)}, u32[]{:S(2)}) collective-permute-start(bf16[512,384]{1,0:T(8,128)(2,1)} %collective-permute-done.6.refs_8_), channel_id=1, source_target_pairs={{0,56},{4,60},{8,0},{12,4},{16,8},{20,12},{24,16},{28,20},{32,24},... | collective-permute-start | bytes 1179656 | tf_op jit(solution)/shard_map/ppermute | solution.py:64
  56.6 2.1 collective-permute-start.7
  58.7 0.5 collective-permute-start.9
  59.2 5.1 %collective-permute-done.12.refs_10_ = bf16[512,384]{1,0:T(8,128)(2,1)S(1)} collective-permute-done((bf16[512,384]{1,0:T(8,128)(2,1)}, bf16[512,384]{1,0:T(8,128)(2,1)S(1)}, u32[]{:S(2)}, u32[]{:S(2)}) %collective-permute-start.12) | collective-permute-done | bytes 393248 | tf_op jit(solution)/shard_map/ppermute | solution.py:64
  64.4 2.5 %collective-permute-start.10 = (bf16[512,384]{1,0:T(8,128)(2,1)}, bf16[512,384]{1,0:T(8,128)(2,1)S(1)}, u32[]{:S(2)}, u32[]{:S(2)}) collective-permute-start(bf16[512,384]{1,0:T(8,128)(2,1)} %collective-permute-done.5.refs_6_), channel_id=1, source_target_pairs={{0,4},{4,0},{8,12},{12,8},{16,20},{20,16},{24,28},{28,24},{32,36},... | collective-permute-start | bytes 1179656 | tf_op jit(solution)/shard_map/ppermute | solution.py:64
  67.3 0.6 collective-permute-start.13
  68.4 2.4 %collective-permute-start.18 = (bf16[256,384]{1,0:T(8,128)(2,1)S(1)}, bf16[256,384]{1,0:T(8,128)(2,1)S(1)}, u32[]{:S(2)}, u32[]{:S(2)}) collective-permute-start(bf16[256,384]{1,0:T(8,128)(2,1)S(1)} %slice.9), channel_id=1, source_target_pairs={{0,56},{4,60},{8,0},{12,4},{16,8},{20,12},{24,16},{28,20},{32,24},... | collective-permute-start | bytes 589832 | tf_op jit(solution)/shard_map/ppermute | solution.py:64
  70.8 3.6 %collective-permute-done.16.refs_14_ = bf16[256,384]{1,0:T(8,128)(2,1)S(1)} collective-permute-done((bf16[256,384]{1,0:T(8,128)(2,1)S(1)}, bf16[256,384]{1,0:T(8,128)(2,1)S(1)}, u32[]{:S(2)}, u32[]{:S(2)}) %collective-permute-start.16) | collective-permute-done | bytes 196640 | tf_op jit(solution)/shard_map/ppermute | solution.py:64
  74.5 1.3 collective-permute-start.17
  76.0 0.9 collective-permute-done.17.refs_15_
  77.3 6.8 %shard_map.104 = (f32[64,8,128]{2,1,0:T(8,128)S(1)}, bf16[8192,384]{1,0:T(8,128)(2,1)S(1)}) custom-call(s32[64]{0:T(128)S(1)} %get-tuple-element.39.order_ref, s32[2]{0:T(128)S(1)} %get-tuple-element.40.size_ref, s32[256]{0:T(256)S(1)} %get-tuple-element.41.at_ref, bf16[1024,384]{1,0:T(8,128)(2,1)S(1)} %fusion.3.kv_ref, ...), custom_call_target="tpu_custom_call" | custom-call | tf_op jit(solution)/shard_map/pallas_call | solution.py:338
  84.1 19.2 %all_to_all.37.st_ref = f32[64,8,128]{2,1,0:T(8,128)S(1)} all-to-all(f32[64,8,128]{2,1,0:T(8,128)S(1)} %get-tuple-element.46), channel_id=1, replica_groups=mesh['frames'=64,'mp'=4] {'frames'}, dimensions={0} | all-to-all | bytes 524288 | tf_op jit(solution)/shard_map/all_to_all | solution.py:346
  103.7 17.8 %all_to_all.38.st_ref = f32[64,8,128]{2,1,0:T(8,128)S(1)} all-to-all(f32[64,8,128]{2,1,0:T(8,128)S(1)} %shard_map.105), channel_id=1, replica_groups=mesh['frames'=64,'mp'=4] {'frames'}, dimensions={0} | all-to-all | bytes 524288 | tf_op jit(solution)/shard_map/all_to_all | solution.py:348
  121.5 10.9 %shard_map.106 = (bf16[4096,384]{1,0:T(8,128)(2,1)S(1)}, bf16[1024,384]{1,0:T(8,128)(2,1)S(1)}) custom-call(s32[64]{0:T(128)S(1)} %get-tuple-element.39.order_ref, s32[2]{0:T(128)S(1)} %get-tuple-element.40.size_ref, s32[256]{0:T(256)S(1)} %get-tuple-element.41.at_ref, bf16[1024,384]{1,0:T(8,128)(2,1)S(1)} %copy-done.3, ...), custom_call_target="tpu_custom_call" | custom-call | tf_op jit(solution)/shard_map/pallas_call | solution.py:349
  132.4 1.7 copy-done.1
  134.0 7.9 %all-to-all-start.4 = ((bf16[64,64,384]{2,1,0:T(8,128)(2,1)}), bf16[64,64,384]{2,1,0:T(8,128)(2,1)}, u32[]{:S(2)}, u32[]{:S(2)}) async-start(bf16[64,64,384]{2,1,0:T(8,128)(2,1)} %bitcast.36), calls=%async_computation.4 | async-start | bytes 6291456 | tf_op jit(solution)/shard_map/all_to_all | solution.py:361
  142.0 0.9 copy.76
  142.9 1.9 copy.75
  144.9 2.3 fusion.8
  147.1 1.3 collective-permute-start.23
  148.4 2.6 %collective-permute-start.24 = (bf16[192,384]{1,0:T(8,128)(2,1)}, bf16[192,384]{1,0:T(8,128)(2,1)}, u32[]{:S(2)}, u32[]{:S(2)}) collective-permute-start(bf16[192,384]{1,0:T(8,128)(2,1)} %get-tuple-element.65), channel_id=1, source_target_pairs={{0,2},{1,3},{2,0},{3,1},{4,6},{5,7},{6,4},{7,5},{8,10},{9,11},{10,... | collective-permute-start | bytes 442376 | tf_op jit(solution)/shard_map/ppermute | solution.py:268
  151.2 1.6 convolution_convert_fusion.1
  152.9 1.4 collective-permute-start.22
  154.3 1.6 convolution_convert_fusion.2
  156.0 0.6 convolution_convert_fusion.3
  156.6 0.6 collective-permute-start.20
  157.2 1.4 and_convert_fusion
  158.6 8.4 %collective-permute-done.22 = bf16[1024,288]{0,1:T(8,128)(2,1)S(1)} collective-permute-done((bf16[1024,288]{0,1:T(8,128)(2,1)S(1)}, bf16[1024,288]{0,1:T(8,128)(2,1)S(1)}, u32[]{:S(2)}, u32[]{:S(2)}) %collective-permute-start.22) | collective-permute-done | bytes 589856 | tf_op jit(solution)/shard_map/ppermute | solution.py:268
  167.0 2.3 %collective-permute-start.25 = (bf16[192,384]{1,0:T(8,128)(2,1)}, bf16[192,384]{1,0:T(8,128)(2,1)}, u32[]{:S(2)}, u32[]{:S(2)}) collective-permute-start(bf16[192,384]{1,0:T(8,128)(2,1)} %get-tuple-element.62), channel_id=1, source_target_pairs={{0,3},{1,0},{2,1},{3,2},{4,7},{5,4},{6,5},{7,6},{8,11},{9,8},{10,9... | collective-permute-start | bytes 442376 | tf_op jit(solution)/shard_map/ppermute | solution.py:268
  169.3 1.7 collective-permute-done.21
  171.0 14.4 %collective-permute-done.20 = bf16[1024,288]{0,1:T(8,128)(2,1)S(1)} collective-permute-done((bf16[1024,288]{0,1:T(8,128)(2,1)S(1)}, bf16[1024,288]{0,1:T(8,128)(2,1)S(1)}, u32[]{:S(2)}, u32[]{:S(2)}) %collective-permute-start.20) | collective-permute-done | bytes 589856 | tf_op jit(solution)/shard_map/ppermute | solution.py:268
  185.4 1.6 fusion.2
  187.0 2.2 copy.74
  189.2 26.2 %all-to-all-done.4 = bf16[64,64,384]{2,1,0:T(8,128)(2,1)} async-done(((bf16[64,64,384]{2,1,0:T(8,128)(2,1)}), bf16[64,64,384]{2,1,0:T(8,128)(2,1)}, u32[]{:S(2)}, u32[]{:S(2)}) %all-to-all-start.4) | async-done | bytes 3145760 | tf_op jit(solution)/shard_map/all_to_all | solution.py:361
  215.4 2.9 %convolution_convert_fusion.4.refs_0_ = bf16[128,384]{1,0:T(8,128)(2,1)S(1)} fusion(bf16[128,4096]{1,0:T(8,128)(2,1)} %and_convert_fusion, bf16[4096,384]{1,0:T(8,128)(2,1)} %bitcast.15), kind=kOutput, calls=%fused_computation.10 | convolution fusion | flops 402702336 | bytes 4292608 | tf_op jit(solution)/shard_map/dot_general | solution.py:384
  218.4 1.4 collective-permute-start.26
  219.7 2.6 %collective-permute-start.27 = (bf16[128,384]{1,0:T(8,128)(2,1)S(1)}, bf16[128,384]{1,0:T(8,128)(2,1)S(1)}, u32[]{:S(2)}, u32[]{:S(2)}) collective-permute-start(bf16[128,384]{1,0:T(8,128)(2,1)S(1)} %convolution_convert_fusion.4.refs_0_), channel_id=1, source_target_pairs={{0,2},{1,3},{2,0},{3,1},{4,6},{5,7},{6,4},{7,5},{8,10},{9,11},{10,... | collective-permute-start | bytes 294920 | tf_op jit(solution)/shard_map/ppermute | solution.py:268
  222.3 1.1 collective-permute-start.28
  223.4 0.5 collective-permute-done.26.refs_1_
  223.9 3.2 %collective-permute-done.27.refs_2_ = bf16[128,384]{1,0:T(8,128)(2,1)S(1)} collective-permute-done((bf16[128,384]{1,0:T(8,128)(2,1)S(1)}, bf16[128,384]{1,0:T(8,128)(2,1)S(1)}, u32[]{:S(2)}, u32[]{:S(2)}) %collective-permute-start.27) | collective-permute-done | bytes 98336 | tf_op jit(solution)/shard_map/ppermute | solution.py:268
  227.1 2.0 shard_map.107
  (81 shorter events, 4.6 us)
Async XLA Ops:
  0.6 19.1 %copy-start = (bf16[16,64,1152]{2,1,0:T(8,128)(2,1)S(1)}, bf16[16,64,1152]{2,1,0:T(8,128)(2,1)}, u32[]{:S(2)}) copy-start(bf16[16,64,1152]{2,1,0:T(8,128)(2,1)} %param.8) | copy-start | bytes 7077892
  0.6 18.9 %copy-start.11 = (bf16[1152,192]{0,1:T(8,128)(2,1)S(1)}, bf16[1152,192]{0,1:T(8,128)(2,1)}, u32[]{:S(2)}) copy-start(bf16[1152,192]{0,1:T(8,128)(2,1)} %param.12) | copy-start | bytes 1327108
  0.7 19.0 %copy-start.12 = (bf16[1152,192]{0,1:T(8,128)(2,1)S(1)}, bf16[1152,192]{0,1:T(8,128)(2,1)}, u32[]{:S(2)}) copy-start(bf16[1152,192]{0,1:T(8,128)(2,1)} %param.13) | copy-start | bytes 1327108
  2.2 17.5 %copy-start.7 = (bf16[128,192]{1,0:T(8,128)(2,1)}, bf16[128,192]{1,0:T(8,128)(2,1)S(1)}, u32[]{:S(2)}) copy-start(bf16[128,192]{1,0:T(8,128)(2,1)S(1)} %copy.64) | copy-start | bytes 147460
  3.7 0.6 copy-start.9
  4.4 16.8 %collective-permute-start.2 = (bf16[128,384]{1,0:T(8,128)(2,1)S(1)}, bf16[128,384]{1,0:T(8,128)(2,1)S(1)}, u32[]{:S(2)}, u32[]{:S(2)}) collective-permute-start(bf16[128,384]{1,0:T(8,128)(2,1)S(1)} %pad_maximum_fusion.1), channel_id=1, source_target_pairs={{0,192},{4,196},{8,200},{12,204},{16,208},{20,212},{24,216},{28,22... | collective-permute-start | bytes 294920 | tf_op jit(solution)/shard_map/ppermute | solution.py:64
  7.8 13.4 %collective-permute-start.1 = (bf16[128,384]{1,0:T(8,128)(2,1)S(1)}, bf16[128,384]{1,0:T(8,128)(2,1)}, u32[]{:S(2)}, u32[]{:S(2)}) collective-permute-start(bf16[128,384]{1,0:T(8,128)(2,1)S(1)} %pad_maximum_fusion.1), channel_id=1, source_target_pairs={{0,128},{4,132},{8,136},{12,140},{16,144},{20,148},{24,152},{28,15... | collective-permute-start | bytes 294920 | tf_op jit(solution)/shard_map/ppermute | solution.py:64
  8.3 13.6 %collective-permute-start = (bf16[128,384]{1,0:T(8,128)(2,1)S(1)}, bf16[128,384]{1,0:T(8,128)(2,1)}, u32[]{:S(2)}, u32[]{:S(2)}) collective-permute-start(bf16[128,384]{1,0:T(8,128)(2,1)S(1)} %pad_maximum_fusion.1), channel_id=1, source_target_pairs={{0,64},{4,68},{8,72},{12,76},{16,80},{20,84},{24,88},{28,92},{32,9... | collective-permute-start | bytes 294920 | tf_op jit(solution)/shard_map/ppermute | solution.py:64
  10.1 0.5 copy-start.14
  11.4 14.7 %all-to-all-start = ((s32[8,1,16]{2,1,0:T(1,128)}), s32[8,1,16]{2,1,0:T(1,128)S(1)}, u32[]{:S(2)}, u32[]{:S(2)}) async-start(s32[8,1,16]{2,1,0:T(1,128)} %copy.66), calls=%async_computation | async-start | bytes 8192 | tf_op jit(solution)/shard_map/all_to_all | solution.py:311
  19.7 1.5 copy-start.4
  19.7 2.2 copy-start.8
  19.7 2.2 copy-start.10
  21.2 62.9 %copy-start.2 = (bf16[1024,384]{1,0:T(8,128)(2,1)}, bf16[1024,384]{1,0:T(8,128)(2,1)S(1)}, u32[]{:S(2)}) copy-start(bf16[1024,384]{1,0:T(8,128)(2,1)S(1)} %fusion.3.kv_ref) | copy-start | bytes 2359300
  21.2 0.7 copy-start.13
  26.1 16.1 %collective-permute-start.3 = (bf16[512,384]{1,0:T(8,128)(2,1)S(1)}, bf16[512,384]{1,0:T(8,128)(2,1)}, u32[]{:S(2)}, u32[]{:S(2)}) collective-permute-start(bf16[512,384]{1,0:T(8,128)(2,1)S(1)} %pad_maximum_fusion.refs_0_), channel_id=1, source_target_pairs={{0,8},{4,12},{8,16},{12,20},{16,24},{20,28},{24,32},{28,36},{32,40... | collective-permute-start | bytes 1179656 | tf_op jit(solution)/shard_map/ppermute | solution.py:64
  26.4 15.8 %collective-permute-start.4 = (bf16[512,384]{1,0:T(8,128)(2,1)S(1)}, bf16[512,384]{1,0:T(8,128)(2,1)}, u32[]{:S(2)}, u32[]{:S(2)}) collective-permute-start(bf16[512,384]{1,0:T(8,128)(2,1)S(1)} %pad_maximum_fusion.refs_0_), channel_id=1, source_target_pairs={{0,56},{4,60},{8,0},{12,4},{16,8},{20,12},{24,16},{28,20},{32,24},... | collective-permute-start | bytes 1179656 | tf_op jit(solution)/shard_map/ppermute | solution.py:64
  42.2 11.6 %collective-permute-start.5 = (bf16[512,384]{1,0:T(8,128)(2,1)}, bf16[512,384]{1,0:T(8,128)(2,1)}, u32[]{:S(2)}, u32[]{:S(2)}) collective-permute-start(bf16[512,384]{1,0:T(8,128)(2,1)} %collective-permute-done.3.refs_2_), channel_id=1, source_target_pairs={{0,8},{4,12},{8,16},{12,20},{16,24},{20,28},{24,32},{28,36},{32,40... | collective-permute-start | bytes 1179656 | tf_op jit(solution)/shard_map/ppermute | solution.py:64
  42.3 11.5 %collective-permute-start.6 = (bf16[512,384]{1,0:T(8,128)(2,1)}, bf16[512,384]{1,0:T(8,128)(2,1)}, u32[]{:S(2)}, u32[]{:S(2)}) collective-permute-start(bf16[512,384]{1,0:T(8,128)(2,1)} %collective-permute-done.4.refs_4_), channel_id=1, source_target_pairs={{0,56},{4,60},{8,0},{12,4},{16,8},{20,12},{24,16},{28,20},{32,24},... | collective-permute-start | bytes 1179656 | tf_op jit(solution)/shard_map/ppermute | solution.py:64
  53.9 10.5 %collective-permute-start.12 = (bf16[512,384]{1,0:T(8,128)(2,1)}, bf16[512,384]{1,0:T(8,128)(2,1)S(1)}, u32[]{:S(2)}, u32[]{:S(2)}) collective-permute-start(bf16[512,384]{1,0:T(8,128)(2,1)} %collective-permute-done.5.refs_6_), channel_id=1, source_target_pairs={{0,8},{4,12},{8,16},{12,20},{16,24},{20,28},{24,32},{28,36},{32,40... | collective-permute-start | bytes 1179656 | tf_op jit(solution)/shard_map/ppermute | solution.py:64
  53.9 13.0 %collective-permute-start.14 = (bf16[512,384]{1,0:T(8,128)(2,1)}, bf16[512,384]{1,0:T(8,128)(2,1)S(1)}, u32[]{:S(2)}, u32[]{:S(2)}) collective-permute-start(bf16[512,384]{1,0:T(8,128)(2,1)} %collective-permute-done.6.refs_8_), channel_id=1, source_target_pairs={{0,56},{4,60},{8,0},{12,4},{16,8},{20,12},{24,16},{28,20},{32,24},... | collective-permute-start | bytes 1179656 | tf_op jit(solution)/shard_map/ppermute | solution.py:64
  56.6 10.4 %collective-permute-start.7 = (bf16[512,384]{1,0:T(8,128)(2,1)S(1)}, bf16[512,384]{1,0:T(8,128)(2,1)S(1)}, u32[]{:S(2)}, u32[]{:S(2)}) collective-permute-start(bf16[512,384]{1,0:T(8,128)(2,1)S(1)} %pad_maximum_fusion.refs_0_), channel_id=1, source_target_pairs={{0,4},{4,0},{8,12},{12,8},{16,20},{20,16},{24,28},{28,24},{32,36},... | collective-permute-start | bytes 1179656 | tf_op jit(solution)/shard_map/ppermute | solution.py:64
  58.7 8.6 %collective-permute-start.8 = (bf16[512,384]{1,0:T(8,128)(2,1)}, bf16[512,384]{1,0:T(8,128)(2,1)S(1)}, u32[]{:S(2)}, u32[]{:S(2)}) collective-permute-start(bf16[512,384]{1,0:T(8,128)(2,1)} %collective-permute-done.3.refs_2_), channel_id=1, source_target_pairs={{0,4},{4,0},{8,12},{12,8},{16,20},{20,16},{24,28},{28,24},{32,36},... | collective-permute-start | bytes 1179656 | tf_op jit(solution)/shard_map/ppermute | solution.py:64
  58.7 9.2 %collective-permute-start.9 = (bf16[512,384]{1,0:T(8,128)(2,1)}, bf16[512,384]{1,0:T(8,128)(2,1)S(1)}, u32[]{:S(2)}, u32[]{:S(2)}) collective-permute-start(bf16[512,384]{1,0:T(8,128)(2,1)} %collective-permute-done.4.refs_4_), channel_id=1, source_target_pairs={{0,4},{4,0},{8,12},{12,8},{16,20},{20,16},{24,28},{28,24},{32,36},... | collective-permute-start | bytes 1179656 | tf_op jit(solution)/shard_map/ppermute | solution.py:64
  64.4 4.1 %collective-permute-start.10 = (bf16[512,384]{1,0:T(8,128)(2,1)}, bf16[512,384]{1,0:T(8,128)(2,1)S(1)}, u32[]{:S(2)}, u32[]{:S(2)}) collective-permute-start(bf16[512,384]{1,0:T(8,128)(2,1)} %collective-permute-done.5.refs_6_), channel_id=1, source_target_pairs={{0,4},{4,0},{8,12},{12,8},{16,20},{20,16},{24,28},{28,24},{32,36},... | collective-permute-start | bytes 1179656 | tf_op jit(solution)/shard_map/ppermute | solution.py:64
  66.9 9.1 %collective-permute-start.11 = (bf16[512,384]{1,0:T(8,128)(2,1)}, bf16[512,384]{1,0:T(8,128)(2,1)S(1)}, u32[]{:S(2)}, u32[]{:S(2)}) collective-permute-start(bf16[512,384]{1,0:T(8,128)(2,1)} %collective-permute-done.6.refs_8_), channel_id=1, source_target_pairs={{0,4},{4,0},{8,12},{12,8},{16,20},{20,16},{24,28},{28,24},{32,36},... | collective-permute-start | bytes 1179656 | tf_op jit(solution)/shard_map/ppermute | solution.py:64
  67.0 7.4 %collective-permute-start.16 = (bf16[256,384]{1,0:T(8,128)(2,1)S(1)}, bf16[256,384]{1,0:T(8,128)(2,1)S(1)}, u32[]{:S(2)}, u32[]{:S(2)}) collective-permute-start(bf16[256,384]{1,0:T(8,128)(2,1)S(1)} %slice.8), channel_id=1, source_target_pairs={{0,8},{4,12},{8,16},{12,20},{16,24},{20,28},{24,32},{28,36},{32,40... | collective-permute-start | bytes 589832 | tf_op jit(solution)/shard_map/ppermute | solution.py:64
  67.3 8.6 %collective-permute-start.13 = (bf16[512,384]{1,0:T(8,128)(2,1)S(1)}, bf16[512,384]{1,0:T(8,128)(2,1)S(1)}, u32[]{:S(2)}, u32[]{:S(2)}) collective-permute-start(bf16[512,384]{1,0:T(8,128)(2,1)S(1)} %collective-permute-done.12.refs_10_), channel_id=1, source_target_pairs={{0,4},{4,0},{8,12},{12,8},{16,20},{20,16},{24,28},{28,24},{32,36},... | collective-permute-start | bytes 1179656 | tf_op jit(solution)/shard_map/ppermute | solution.py:64
  67.9 8.1 %collective-permute-start.15 = (bf16[512,384]{1,0:T(8,128)(2,1)S(1)}, bf16[512,384]{1,0:T(8,128)(2,1)S(1)}, u32[]{:S(2)}, u32[]{:S(2)}) collective-permute-start(bf16[512,384]{1,0:T(8,128)(2,1)S(1)} %collective-permute-done.14.refs_12_), channel_id=1, source_target_pairs={{0,4},{4,0},{8,12},{12,8},{16,20},{20,16},{24,28},{28,24},{32,36},... | collective-permute-start | bytes 1179656 | tf_op jit(solution)/shard_map/ppermute | solution.py:64
  68.4 7.4 %collective-permute-start.18 = (bf16[256,384]{1,0:T(8,128)(2,1)S(1)}, bf16[256,384]{1,0:T(8,128)(2,1)S(1)}, u32[]{:S(2)}, u32[]{:S(2)}) collective-permute-start(bf16[256,384]{1,0:T(8,128)(2,1)S(1)} %slice.9), channel_id=1, source_target_pairs={{0,56},{4,60},{8,0},{12,4},{16,8},{20,12},{24,16},{28,20},{32,24},... | collective-permute-start | bytes 589832 | tf_op jit(solution)/shard_map/ppermute | solution.py:64
  74.5 2.4 %collective-permute-start.17 = (bf16[256,384]{1,0:T(8,128)(2,1)S(1)}, bf16[256,384]{1,0:T(8,128)(2,1)S(1)}, u32[]{:S(2)}, u32[]{:S(2)}) collective-permute-start(bf16[256,384]{1,0:T(8,128)(2,1)S(1)} %collective-permute-done.16.refs_14_), channel_id=1, source_target_pairs={{0,4},{4,0},{8,12},{12,8},{16,20},{20,16},{24,28},{28,24},{32,36},... | collective-permute-start | bytes 589832 | tf_op jit(solution)/shard_map/ppermute | solution.py:64
  75.8 1.4 collective-permute-start.19
  84.1 37.4 %copy-start.3 = (bf16[1024,384]{1,0:T(8,128)(2,1)S(1)}, bf16[1024,384]{1,0:T(8,128)(2,1)}, u32[]{:S(2)}) copy-start(bf16[1024,384]{1,0:T(8,128)(2,1)} %copy-done.2) | copy-start | bytes 2359300
  132.4 1.7 copy-start.1
  134.0 8.0 %copy-start.6 = (bf16[768,192]{0,1:T(8,128)(2,1)S(1)}, bf16[768,192]{0,1:T(8,128)(2,1)}, u32[]{:S(2)}) copy-start(bf16[768,192]{0,1:T(8,128)(2,1)} %param.11) | copy-start | bytes 884740
  134.0 81.4 %all-to-all-start.4 = ((bf16[64,64,384]{2,1,0:T(8,128)(2,1)}), bf16[64,64,384]{2,1,0:T(8,128)(2,1)}, u32[]{:S(2)}, u32[]{:S(2)}) async-start(bf16[64,64,384]{2,1,0:T(8,128)(2,1)} %bitcast.36), calls=%async_computation.4 | async-start | bytes 6291456 | tf_op jit(solution)/shard_map/all_to_all | solution.py:361
  147.1 42.1 %collective-permute-start.23 = (bf16[192,384]{1,0:T(8,128)(2,1)}, bf16[192,384]{1,0:T(8,128)(2,1)S(1)}, u32[]{:S(2)}, u32[]{:S(2)}) collective-permute-start(bf16[192,384]{1,0:T(8,128)(2,1)} %get-tuple-element.64), channel_id=1, source_target_pairs={{0,1},{1,2},{2,3},{3,0},{4,5},{5,6},{6,7},{7,4},{8,9},{9,10},{10,1... | collective-permute-start | bytes 442376 | tf_op jit(solution)/shard_map/ppermute | solution.py:268
  148.4 40.8 %collective-permute-start.24 = (bf16[192,384]{1,0:T(8,128)(2,1)}, bf16[192,384]{1,0:T(8,128)(2,1)}, u32[]{:S(2)}, u32[]{:S(2)}) collective-permute-start(bf16[192,384]{1,0:T(8,128)(2,1)} %get-tuple-element.65), channel_id=1, source_target_pairs={{0,2},{1,3},{2,0},{3,1},{4,6},{5,7},{6,4},{7,5},{8,10},{9,11},{10,... | collective-permute-start | bytes 442376 | tf_op jit(solution)/shard_map/ppermute | solution.py:268
  151.2 4.9 %copy-start.5 = (bf16[1152,384]{0,1:T(8,128)(2,1)S(1)}, bf16[1152,384]{0,1:T(8,128)(2,1)}, u32[]{:S(2)}) copy-start(bf16[1152,384]{0,1:T(8,128)(2,1)} %copy-done.4) | copy-start | bytes 2654212
  152.9 14.1 %collective-permute-start.22 = (bf16[1024,288]{0,1:T(8,128)(2,1)S(1)}, bf16[1024,288]{0,1:T(8,128)(2,1)S(1)}, u32[]{:S(2)}, u32[]{:S(2)}) collective-permute-start(bf16[1024,288]{0,1:T(8,128)(2,1)S(1)} %convolution_convert_fusion.1), channel_id=1, source_target_pairs={{0,3},{1,0},{2,1},{3,2},{4,7},{5,4},{6,5},{7,6},{8,11},{9,8},{10,9... | collective-permute-start | bytes 1769480 | tf_op jit(solution)/shard_map/ppermute | solution.py:268
  155.8 15.2 %collective-permute-start.21 = (bf16[1024,288]{0,1:T(8,128)(2,1)S(1)}, bf16[1024,288]{0,1:T(8,128)(2,1)S(1)}, u32[]{:S(2)}, u32[]{:S(2)}) collective-permute-start(bf16[1024,288]{0,1:T(8,128)(2,1)S(1)} %convolution_convert_fusion.2), channel_id=1, source_target_pairs={{0,2},{1,3},{2,0},{3,1},{4,6},{5,7},{6,4},{7,5},{8,10},{9,11},{10,... | collective-permute-start | bytes 1769480 | tf_op jit(solution)/shard_map/ppermute | solution.py:268
  156.6 28.8 %collective-permute-start.20 = (bf16[1024,288]{0,1:T(8,128)(2,1)S(1)}, bf16[1024,288]{0,1:T(8,128)(2,1)S(1)}, u32[]{:S(2)}, u32[]{:S(2)}) collective-permute-start(bf16[1024,288]{0,1:T(8,128)(2,1)S(1)} %convolution_convert_fusion.3), channel_id=1, source_target_pairs={{0,1},{1,2},{2,3},{3,0},{4,5},{5,6},{6,7},{7,4},{8,9},{9,10},{10,1... | collective-permute-start | bytes 1769480 | tf_op jit(solution)/shard_map/ppermute | solution.py:268
  167.0 22.2 %collective-permute-start.25 = (bf16[192,384]{1,0:T(8,128)(2,1)}, bf16[192,384]{1,0:T(8,128)(2,1)}, u32[]{:S(2)}, u32[]{:S(2)}) collective-permute-start(bf16[192,384]{1,0:T(8,128)(2,1)} %get-tuple-element.62), channel_id=1, source_target_pairs={{0,3},{1,0},{2,1},{3,2},{4,7},{5,4},{6,5},{7,6},{8,11},{9,8},{10,9... | collective-permute-start | bytes 442376 | tf_op jit(solution)/shard_map/ppermute | solution.py:268
  218.4 5.6 %collective-permute-start.26 = (bf16[128,384]{1,0:T(8,128)(2,1)S(1)}, bf16[128,384]{1,0:T(8,128)(2,1)S(1)}, u32[]{:S(2)}, u32[]{:S(2)}) collective-permute-start(bf16[128,384]{1,0:T(8,128)(2,1)S(1)} %convolution_convert_fusion.4.refs_0_), channel_id=1, source_target_pairs={{0,1},{1,2},{2,3},{3,0},{4,5},{5,6},{6,7},{7,4},{8,9},{9,10},{10,1... | collective-permute-start | bytes 294920 | tf_op jit(solution)/shard_map/ppermute | solution.py:268
  219.7 7.4 %collective-permute-start.27 = (bf16[128,384]{1,0:T(8,128)(2,1)S(1)}, bf16[128,384]{1,0:T(8,128)(2,1)S(1)}, u32[]{:S(2)}, u32[]{:S(2)}) collective-permute-start(bf16[128,384]{1,0:T(8,128)(2,1)S(1)} %convolution_convert_fusion.4.refs_0_), channel_id=1, source_target_pairs={{0,2},{1,3},{2,0},{3,1},{4,6},{5,7},{6,4},{7,5},{8,10},{9,11},{10,... | collective-permute-start | bytes 294920 | tf_op jit(solution)/shard_map/ppermute | solution.py:268
  222.3 4.8 %collective-permute-start.28 = (bf16[128,384]{1,0:T(8,128)(2,1)S(1)}, bf16[128,384]{1,0:T(8,128)(2,1)S(1)}, u32[]{:S(2)}, u32[]{:S(2)}) collective-permute-start(bf16[128,384]{1,0:T(8,128)(2,1)S(1)} %convolution_convert_fusion.4.refs_0_), channel_id=1, source_target_pairs={{0,3},{1,0},{2,1},{3,2},{4,7},{5,4},{6,5},{7,6},{8,11},{9,8},{10,9... | collective-permute-start | bytes 294920 | tf_op jit(solution)/shard_map/ppermute | solution.py:268
